TPU v7x, 128 devices: a whole 4x4x4 slice. The times are simulated.
128 devices in a mesh: row: 32 (over x, y, core), col: 4 (over z).
Axes of the slice: x: 4, y: 4, z: 4, core: 2. Of those that a mesh axis runs over, the one named last changes fastest.
Arguments:
- design: float32 [256, 1048576], P('col', 'row'), may hold values from -6 to 6
- sign_bits: int32 [1048576], P('row'), may hold values from 0 to 1
- picks: int32 [2048], replicated, may hold values from 0 to 1048575
- owners: int32 [2048, 1], replicated, may hold values from 0 to 31; in each aligned block of 2048 rows (0 to 2047, 2048 to 4095, ...) at most 128 rows name the same one
Outputs:
- sketch: float32 [256, 4096], P('col', 'row')
Inputs may be any that keep to these rules, and one draw needn't show every extreme that they name: `owners`: no owner is named by more than 128 samples, a bound that some block reaches.
All inputs are finite; a program needn't handle non-finite values.
Results may differ from a plain program's by a relative error of at most 0.000071.
Values sent between devices are 32-bit elements; how exact they have to be, the bound alone decides.
No kernel may reach another device: no remote copies, remote signals or barrier semaphores. Data moves between devices by JAX's collectives and lax.ppermute only.
A program may use at most 128 MiB of HBM per device.

v0:
```python
import math

import jax
import jax.numpy as jnp
from jax import lax
from jax.sharding import PartitionSpec as P


def parity_bits(anded, nbits):
    count = jnp.zeros_like(anded)
    for place in range(nbits):
        count = count ^ anded >> place & 1
    return count


def sylvester(order):
    index = jnp.arange(order, dtype=jnp.int32)
    anded = index[:, None] & index[None, :]
    return (1 - 2 * parity_bits(anded, max(order.bit_length(), 1))).astype(jnp.float32)


def slot_table(owners, groups, capacity):
    owner_col = owners[:, 0]
    onehot = (owner_col[:, None] == jnp.arange(groups, dtype=jnp.int32)[None, :]).astype(jnp.int32)
    before = jnp.cumsum(onehot, axis=0) - onehot
    return owner_col * capacity + jnp.sum(before * onehot, axis=1)


def shards(design, sign_bits, picks, owners):
    width, rows_here = design.shape
    groups = lax.axis_size("row")
    samples = picks.shape[0]
    capacity = 2 * (samples // groups)
    blocks = rows_here // 128
    highest = lax.Precision.HIGHEST
    signs = (1 - 2 * sign_bits).astype(jnp.float32)
    scale = jnp.float32(1.0 / math.sqrt(rows_here * groups))
    mixed = design * signs[None, :]
    shaped = mixed.reshape(width, blocks, 128)
    inner = jnp.einsum("cab,bk->cak", shaped, sylvester(128), precision=highest)
    local = jnp.einsum("cak,aj->cjk", inner, sylvester(blocks), precision=highest)
    local = local.reshape(width, rows_here) * scale
    me = lax.axis_index("row")
    source = picks // rows_here
    offset = picks % rows_here
    table = sylvester(groups)
    spread = local.reshape(width, groups, rows_here // groups)
    merged = jnp.einsum(
        "cdt,dj->cjt",
        lax.all_to_all(spread, "row", split_axis=1, concat_axis=1, tiled=True),
        table,
        precision=highest,
    )
    mixing = lax.all_to_all(merged, "row", split_axis=1, concat_axis=1, tiled=True)
    mixing = mixing.reshape(width, rows_here)
    picked = jnp.take(mixing, offset, axis=1)
    values = jnp.where((source == me)[None, :], picked, jnp.float32(0.0))
    slot = slot_table(owners, groups, capacity)
    term = jnp.zeros((width, capacity * groups), jnp.float32).at[:, slot].set(values)
    return lax.psum_scatter(term, "row", scatter_dimension=1, tiled=True)


def solution(mesh):
    placed = (P("col", "row"), P("row"), P(), P())
    return jax.shard_map(
        shards, mesh=mesh, in_specs=placed, out_specs=P("col", "row"), check_vma=False
    )
```

profile of v0, /device:TPU:0, one launch (start us, length us, event | category | flops | bytes accessed | tf_op | source)
XLA Modules:
  0.0 423.0 jit_solution(2888047441964739752)
XLA Ops:
  6.5 0.9 subtract_convert_fusion
  7.5 4.1 multiply_bitcast_fusion.1
  11.5 1.5 copy.20
  13.0 8.5 %fusion.59 = f32[64,256,128]{2,1,0:T(8,128)S(1)} fusion(f32[64,256,128]{2,1,0:T(8,128)S(1)} %bitcast.43), kind=kOutput, calls=%fused_computation.66 | convolution fusion | flops 3221667840 | bytes 16777216 | tf_op jit(solution)/shard_map/cab,bk->cak/dot_general | solution.py:40
  21.5 10.1 %multiply_bitcast_fusion = f32[64,256,128]{2,1,0:T(8,128)} fusion(f32[64,256,128]{2,1,0:T(8,128)S(1)} %fusion.59), kind=kOutput, calls=%fused_computation.4 | convolution fusion | flops 6446514176 | bytes 16777216 | tf_op jit(solution)/shard_map/cak,aj->cjk/dot_general | solution.py:41
  31.6 9.3 %mul.59 = f32[64,32,1024]{2,1,0:T(8,128)} reshape(f32[64,256,128]{2,1,0:T(8,128)} %multiply_bitcast_fusion) | data formatting | bytes 16777216 | tf_op jit(solution)/shard_map/mul | solution.py:42
  40.8 8.2 %copy.13 = f32[64,32,1024]{2,0,1:T(8,128)S(1)} copy(f32[64,32,1024]{2,1,0:T(8,128)} %mul.59) | data formatting | bytes 16777216 | tf_op jit(solution)/shard_map/mul | solution.py:42
  49.1 102.9 %all_to_all.10 = f32[64,32,1024]{2,0,1:T(8,128)S(1)} all-to-all(f32[64,32,1024]{2,0,1:T(8,128)S(1)} %copy.13), channel_id=1, replica_groups=mesh['row'=32,'col'=4] {'row'}, dimensions={1} | all-to-all | bytes 16777216 | tf_op jit(solution)/shard_map/all_to_all | solution.py:50
  151.9 12.6 %fusion.2 = f32[64,32,1024]{2,1,0:T(8,128)S(1)} fusion(f32[64,32,1024]{2,0,1:T(8,128)S(1)} %all_to_all.10), kind=kOutput, calls=%fused_computation.6 | convolution fusion | flops 805327872 | bytes 16777216 | tf_op jit(solution)/shard_map/cdt,dj->cjt/dot_general | solution.py:48
  164.6 8.3 %copy.15 = f32[64,32,1024]{2,0,1:T(8,128)} copy(f32[64,32,1024]{2,1,0:T(8,128)S(1)} %fusion.2) | data formatting | bytes 16777216 | tf_op jit(solution)/shard_map/cdt,dj->cjt/transpose | solution.py:48
  172.9 0.0 copy-start
  172.9 0.0 copy-start.1
  172.9 5.1 %all-to-all-start.1 = ((f32[64,32,1024]{2,0,1:T(8,128)}), f32[64,32,1024]{2,0,1:T(8,128)}, u32[]{:S(2)}, u32[]{:S(2)}) async-start(f32[64,32,1024]{2,0,1:T(8,128)} %copy.15), calls=%async_computation.1 | async-start | bytes 16777216 | tf_op jit(solution)/shard_map/all_to_all | solution.py:54
  178.0 0.0 reduce-scatter.2.cloned.1.call-start
  178.1 0.0 copy-done
  178.1 9.1 %reduce-window.6 = s32[32,16,128]{2,1,0:T(8,128)S(1)} reduce-window(s32[32,16,128]{2,1,0:T(8,128)S(1)} %fusion.49, s32[]{:T(128)} %constant.29.clone.1), window={size=1x1x128 pad=0_0x0_0x127_0}, to_apply=%region_0.1 | reduce-window | flops 8323072 | bytes 524292 | tf_op jit(solution)/shard_map/reduce-window
  187.2 0.1 slice.10
  187.3 0.2 copy.18
  187.6 0.2 reduce-window.9
  187.7 0.1 broadcast_add_fusion
  187.9 0.1 fusion.15
  188.0 0.0 copy-done.1
  188.1 103.2 %all-to-all-done.1 = f32[64,32,1024]{2,0,1:T(8,128)} async-done(((f32[64,32,1024]{2,0,1:T(8,128)}), f32[64,32,1024]{2,0,1:T(8,128)}, u32[]{:S(2)}, u32[]{:S(2)}) %all-to-all-start.1) | async-done | bytes 8388640 | tf_op jit(solution)/shard_map/all_to_all | solution.py:54
  291.3 12.2 %copy.16 = f32[64,32,1024]{0,2,1:T(8,128)} copy(f32[64,32,1024]{2,0,1:T(8,128)} %all-to-all-done.1) | data formatting | bytes 16777216 | tf_op jit(solution)/shard_map/all_to_all | solution.py:54
  303.5 19.9 %scatter_custom_fusion = f32[64,4096]{0,1:T(8,128)} fusion(s32[2048]{0:T(1024)S(1)} %bitcast.51, f32[]{:T(128)} %constant.27.clone.1, f32[]{:T(128)} %constant.57.clone.1, pred[2048]{0:T(1024)(128)(4,1)S(1)} %get-tuple-element.6, pred[2048]{0:T(1024)(128)(4,1)S(1)} %get-tuple-element.5, f32[64,32768]{0,1:T(8,128)} %bitcast.44, s32[2048]{0:T(1024)S(1)} %broadcast_clamp_fusion), kind=kCustom, calls=%fused_computation.7 | custom fusion | flops 262144 | bytes 17839616 | tf_op jit(solution)/shard_map/scatter | solution.py:59
  323.5 0.0 reduce-scatter.2.cloned.1.call-update
  323.5 90.7 %reduce-scatter.2.cloned.1.call-done = f32[64,128]{0,1:T(8,128)} async-done(((f32[64,4096]{0,1:T(8,128)}), f32[64,128]{0,1:T(8,128)}) %reduce-scatter.2.cloned.1.call-update) | async-done | bytes 32784 | tf_op jit(solution)/shard_map/reduce_scatter | solution.py:60
  414.2 1.5 copy.17
  (4 shorter events, 0.1 us)
Async XLA Ops:
  172.9 5.2 %copy-start = (s32[2048,1]{0,1:T(1,128)S(1)}, s32[2048,1]{0,1:T(1,128)}, u32[]{:S(2)}) copy-start(s32[2048,1]{0,1:T(1,128)} %param.7) | copy-start | bytes 24580
  172.9 15.1 %copy-start.1 = (s32[2048]{0:T(1024)S(1)}, s32[2048]{0:T(1024)}, u32[]{:S(2)}) copy-start(s32[2048]{0:T(1024)} %param.6) | copy-start | bytes 24580
  172.9 118.4 %all-to-all-start.1 = ((f32[64,32,1024]{2,0,1:T(8,128)}), f32[64,32,1024]{2,0,1:T(8,128)}, u32[]{:S(2)}, u32[]{:S(2)}) async-start(f32[64,32,1024]{2,0,1:T(8,128)} %copy.15), calls=%async_computation.1 | async-start | bytes 16777216 | tf_op jit(solution)/shard_map/all_to_all | solution.py:54
  178.0 236.2 %reduce-scatter.2.cloned.1.call-start = ((), (), s32[]{:S(2)}) async-start(), calls=%async_computation.3 | async-start | bytes 2162688 | tf_op jit(solution)/shard_map/reduce_scatter | solution.py:60
Sparse Core Ops, SparseCore 0:
  323.6 90.5 reduce-scatter.1
where the time goes:
time: 431 us; the launch traced here: 423 us
  waiting for transfers between devices  194 us (45%)
  blocking collectives  103 us (24%)
  local copies, waits for them, and re-layouts  41.5 us (10%)
  other arithmetic  34.5 us (8%)
  matrix products  31.1 us (7%)
  between operations  14 us (3%)
  starting transfers between devices  5.13 us (1%)
    all_to_all x1, waiting for transfers between devices, shards(): lax.all_to_all(merged, 'row', split_axis=1, concat_axis=1, tiled=True)  103 us
    all_to_all x1, blocking collectives, shards(): lax.all_to_all(spread, 'row', split_axis=1, concat_axis=1, tiled=True)  103 us
    reduce_scatter x1, waiting for transfers between devices, shards(): return lax.psum_scatter(term, 'row', scatter_dimension=1, tiled=True)  90.7 us
    scatter x1, other arithmetic, shards(): jnp.zeros((width, capacity * groups), jnp.float32).at[:, slot].set(values)  19.9 us
    mul x2, local copies, waits for them, and re-layouts, shards(): local = local.reshape(width, rows_here) * scale  17.5 us
    dot_general x1, matrix products, shards(): jnp.einsum('cdt,dj->cjt', lax.all_to_all(spread, 'row', split_axis=1, con...  12.6 us
    all_to_all x1, local copies, waits for them, and re-layouts, shards(): lax.all_to_all(merged, 'row', split_axis=1, concat_axis=1, tiled=True)  12.2 us
    dot_general x1, matrix products, shards(): jnp.einsum('cak,aj->cjk', inner, sylvester(blocks), precision=highest)  10.1 us
  transfers between devices with their start and end apart: 2, of which 2 were waited for; matrix products, arithmetic and copies ran while one was open for 2% of the time, Pallas kernels for 0%

commit v1 on v0

v1 whole, which is shorter than its diff:
```python
import functools

import jax
import jax.numpy as jnp
from jax import lax
from jax.experimental import pallas as pl
from jax.experimental.pallas import tpu as pltpu
from jax.sharding import PartitionSpec as P

LANES = 128
SIDE_X, SIDE_Y = 4, 4
CHUNKS = 8
INNER = 16
DEPTH = 256
CAPACITY = 128
BLOCKS = 32


def parity(value, bits):
    shift = 1
    while shift < bits:
        value = value ^ (value >> shift)
        shift = shift * 2
    return value & 1


def butterflies(values):
    half = 1
    values = list(values)
    while half < len(values):
        for start in range(0, len(values), 2 * half):
            for at in range(start, start + half):
                first, second = values[at], values[at + half]
                values[at], values[at + half] = first + second, first - second
        half = half * 2
    return values


def slot_kernel(me, picks_ref, owners_ref, packed_ref, weight_ref, rows_here):
    core, along_y, along_x = me & 1, (me >> 1) & 3, me >> 3
    shape = (BLOCKS, LANES)
    target = lax.broadcasted_iota(jnp.int32, shape, 0)
    owner = owners_ref[...]
    pick = picks_ref[...]
    rel = (
        (((owner & 1) ^ core) << 4)
        | ((((owner >> 3) - along_x) & 3) << 2)
        | (((owner >> 1) - along_y) & 3)
    )
    source = pick // rows_here
    offset = pick % rows_here
    sign = (1 - 2 * parity(source & me, 8)).astype(jnp.float32)
    column = offset // DEPTH
    odd = column & 1
    row = (column >> 1) * DEPTH + (offset % DEPTH)
    groups = pick.shape[0]
    up = lax.broadcasted_iota(jnp.int32, (LANES, 2 * LANES), 0)
    to = lax.broadcasted_iota(jnp.int32, (LANES, 2 * LANES), 1)
    upper = jnp.where((to >= LANES) | (up < to), 1.0, 0.0).astype(jnp.bfloat16)
    onehot = [
        jnp.where(rel[g:g + 1, :] == target, 1.0, 0.0) for g in range(groups)
    ]
    counted = jnp.dot(
        jnp.concatenate(onehot, axis=0).astype(jnp.bfloat16),
        upper,
        preferred_element_type=jnp.float32,
    )
    base = jnp.zeros(shape, jnp.float32)
    place = lax.broadcasted_iota(jnp.int32, (CAPACITY, LANES), 0)
    total = jnp.zeros((2 * BLOCKS, LANES), jnp.float32)
    for g in range(groups):
        here = counted[g * BLOCKS:(g + 1) * BLOCKS]
        rank = jnp.sum(onehot[g] * (here[:, :LANES] + base), axis=0, keepdims=True)
        base = base + here[:, LANES:]
        rank = rank.astype(jnp.int32)
        packed_ref[g:g + 1, :] = row[g:g + 1] | ((rel[g:g + 1] * CAPACITY + rank) << 14)
        held = onehot[g] * sign[g:g + 1]
        odd_here = odd[g:g + 1].astype(jnp.float32)
        both = jnp.concatenate([held * (1.0 - odd_here), held * odd_here], axis=0)
        at = jnp.where(rank == place, 1.0, 0.0).astype(jnp.bfloat16)
        total = total + lax.dot_general(
            both.astype(jnp.bfloat16), at, (((1,), (1,)), ((), ())),
            preferred_element_type=jnp.float32,
        )
    weight_ref[...] = total * jnp.float32(2.0 ** -10)


def local_kernel(
    x_ref, bits_ref, picks_ref, owners_ref, keep_ref, send_ref,
    x_buf, signs, had, parts, table, packed, listed, weight, rows, x_sem, l_sem,
):
    width = x_ref.shape[0]
    rows_here = x_ref.shape[1]
    span = rows_here // CHUNKS
    me = lax.axis_index("row")

    def chunk_copy(g):
        return pltpu.make_async_copy(
            x_ref.at[:, pl.ds(g * span, span)], x_buf.at[g], x_sem.at[g]
        )

    for g in range(CHUNKS):
        chunk_copy(g).start()

    slot_kernel(me, picks_ref, owners_ref, packed, weight, rows_here)
    listing = pltpu.make_async_copy(packed, listed, l_sem)
    listing.start()
    signs[...] = (1 - 2 * bits_ref[...]).astype(jnp.float32)
    i = lax.broadcasted_iota(jnp.int32, (DEPTH, DEPTH), 0)
    k = lax.broadcasted_iota(jnp.int32, (DEPTH, DEPTH), 1)
    matrix = (1 - 2 * parity(i & k, 8)).astype(jnp.float32).astype(jnp.bfloat16)
    had[:, :DEPTH] = matrix
    had[:, DEPTH:] = matrix

    @pl.loop(0, CHUNKS)
    def _(g):
        chunk_copy(g).wait()
        for half in range(2):
            for c in range(0, width, 16):
                values = []
                for j in range(INNER):
                    at = j * DEPTH + half * LANES
                    sign = signs[pl.ds(g * (span // LANES) + at // LANES, 1), :]
                    values.append(x_buf[g, c:c + 16, at:at + LANES] * sign)
                for j, value in enumerate(butterflies(values)):
                    high = value.astype(jnp.bfloat16)
                    low = (value - high.astype(jnp.float32)).astype(jnp.bfloat16)
                    at = pl.ds(j * width + c, 16)
                    parts[at, half * LANES:(half + 1) * LANES] = high
                    parts[at, DEPTH + half * LANES:DEPTH + (half + 1) * LANES] = low
        for four in range(INNER // 4):
            made = lax.dot_general(
                had[...], parts[four * 4 * width:(four + 1) * 4 * width, :],
                (((1,), (1,)), ((), ())),
                preferred_element_type=jnp.float32,
            )
            at = g * (INNER // 2) + four * 2
            table[pl.ds(at * DEPTH, DEPTH), :] = made[:, :LANES]
            table[pl.ds((at + 1) * DEPTH, DEPTH), :] = made[:, LANES:]

    stretch = table.shape[0] // CHUNKS
    step = 32

    @pl.loop(0, stretch // step)
    def _(at):
        values = [table[pl.ds(g * stretch + at * step, step), :] for g in range(CHUNKS)]
        for g, value in enumerate(butterflies(values)):
            table[pl.ds(g * stretch + at * step, step), :] = value

    listing.wait()

    @pl.loop(0, packed.shape[0])
    def _(g):
        for lane in range(LANES):
            word = listed[g, lane]
            rows[pl.ds(word >> 14, 1), :] = table[pl.ds(word & 16383, 1), :]

    @pl.loop(0, BLOCKS // 2)
    def _(b):
        for out_ref, block in ((keep_ref, b), (send_ref, b + BLOCKS // 2)):
            turned = rows[pl.ds(block * CAPACITY, CAPACITY), :].T
            even = weight[pl.ds(block, 1), :]
            odd = weight[pl.ds(block + BLOCKS, 1), :]
            zero = jnp.zeros((width, CAPACITY), jnp.float32)
            value = jnp.where(even != 0.0, turned[:width] * even, zero)
            value = jnp.where(odd != 0.0, turned[width:] * odd, value)
            out_ref[b] = value


def local_parts(design, bits, picks, owners):
    width, rows_here = design.shape
    vmem = pl.BlockSpec(memory_space=pltpu.VMEM)
    half = jax.ShapeDtypeStruct((BLOCKS // 2, width, CAPACITY), jnp.float32)
    return pl.pallas_call(
        local_kernel,
        out_shape=(half, half),
        in_specs=[pl.BlockSpec(memory_space=pl.ANY), vmem, vmem, vmem],
        out_specs=(vmem, vmem),
        scratch_shapes=[
            pltpu.VMEM((CHUNKS, width, rows_here // CHUNKS), jnp.float32),
            pltpu.VMEM((rows_here // LANES, LANES), jnp.float32),
            pltpu.VMEM((DEPTH, 2 * DEPTH), jnp.bfloat16),
            pltpu.VMEM((INNER * width, 2 * DEPTH), jnp.bfloat16),
            pltpu.VMEM((rows_here // 2, LANES), jnp.float32),
            pltpu.VMEM((16, LANES), jnp.int32),
            pltpu.SMEM((16, LANES), jnp.int32),
            pltpu.VMEM((2 * BLOCKS, LANES), jnp.float32),
            pltpu.VMEM((BLOCKS * CAPACITY, LANES), jnp.float32),
            pltpu.SemaphoreType.DMA((CHUNKS,)),
            pltpu.SemaphoreType.DMA,
        ],
        compiler_params=pltpu.CompilerParams(vmem_limit_bytes=48 << 20),
    )(design, bits, picks, owners)


def place(x, y, core):
    return (x * SIDE_Y + y) * 2 + core


def shift(dx, dy, dcore):
    return [
        (place(x, y, c), place((x + dx) % SIDE_X, (y + dy) % SIDE_Y, c ^ dcore))
        for x in range(SIDE_X)
        for y in range(SIDE_Y)
        for c in range(2)
    ]


def shards(design, sign_bits, picks, owners):
    bits = sign_bits.reshape(-1, LANES)
    keep, send = local_parts(
        design, bits, picks.reshape(-1, LANES), owners.reshape(-1, LANES)
    )
    held = keep + lax.ppermute(send, "row", shift(0, 0, 1))
    own = held[0:4]
    for dx in (1, 2, 3):
        own = own + lax.ppermute(held[dx * 4:dx * 4 + 4], "row", shift(dx, 0, 0))
    out = own[0]
    for dy in (1, 2, 3):
        out = out + lax.ppermute(own[dy], "row", shift(0, dy, 0))
    return out


def solution(mesh):
    placed = (P("col", "row"), P("row"), P(), P())
    return jax.shard_map(
        shards, mesh=mesh, in_specs=placed, out_specs=P("col", "row"), check_vma=False
    )
```

time: 431 us -> 38.4 us (0.09); the launches traced: 423 us -> 38.2 us
  waiting for transfers between devices: 194 us -> 10.8 us
  blocking collectives: 103 us -> 0 us
  local copies, waits for them, and re-layouts: 41.5 us -> 2.33 us
  other arithmetic: 34.5 us -> 0.73 us
  matrix products: 31.1 us -> 0 us
  between operations: 14 us -> 0.05 us
  Pallas kernels: 0 us -> 13.7 us
  starting transfers between devices: 5.13 us -> 10.6 us
    all_to_all x1 -> x0, waiting for transfers between devices: 103 us -> none  [shards(): lax.all_to_all(merged, 'row', split_axis=1, concat_axis=1, tiled=True)]
    all_to_all x1 -> x0, blocking collectives: 103 us -> none  [shards(): lax.all_to_all(spread, 'row', split_axis=1, concat_axis=1, tiled=True)]
    reduce_scatter x1 -> x0, waiting for transfers between devices: 90.7 us -> none  [shards(): return lax.psum_scatter(term, 'row', scatter_dimension=1, tiled=True)]
    dot_general x3 -> x0, matrix products: 31.1 us -> none  [the longest x1 12.6 us: shards(): jnp.einsum('cdt,dj->cjt', lax.all_to_all(spread, 'row', split_axis=1, con...]
    scatter x1 -> x0, other arithmetic: 19.9 us -> none  [shards(): jnp.zeros((width, capacity * groups), jnp.float32).at[:, slot].set(values)]
    mul x2 -> x0, local copies, waits for them, and re-layouts: 17.5 us -> none  [shards(): local = local.reshape(width, rows_here) * scale]
    pallas_call x0 -> x1, Pallas kernels: none -> 13.7 us  [local_parts(): pl.pallas_call(local_kernel, out_shape=(half, half), in_specs=[pl.BlockSp...]
    all_to_all x1 -> x0, local copies, waits for them, and re-layouts: 12.2 us -> none  [shards(): lax.all_to_all(merged, 'row', split_axis=1, concat_axis=1, tiled=True)]
  transfers between devices with their start and end apart: 2 -> 7, of which waited for: 2 -> 6; matrix products, arithmetic and copies ran while one was open for 2% -> 0% of each run, Pallas kernels for 0% -> 0%
where the time goes in v1:
time: 38.4 us; the launch traced here: 38.2 us
  Pallas kernels  13.7 us (36%)
  waiting for transfers between devices  10.8 us (28%)
  starting transfers between devices  10.6 us (28%)
  local copies, waits for them, and re-layouts  2.33 us (6%)
  other arithmetic  0.73 us (2%)
    pallas_call x1, Pallas kernels, local_parts(): pl.pallas_call(local_kernel, out_shape=(half, half), in_specs=[pl.BlockSp...  13.7 us
    ppermute x3, waiting for transfers between devices, shards(): own = own + lax.ppermute(held[dx * 4:dx * 4 + 4], 'row', shift(dx, 0, 0))  5.49 us
    ppermute x3, starting transfers between devices, shards(): out = out + lax.ppermute(own[dy], 'row', shift(0, dy, 0))  5.29 us
    ppermute x3, starting transfers between devices, shards(): own = own + lax.ppermute(held[dx * 4:dx * 4 + 4], 'row', shift(dx, 0, 0))  5.2 us
    ppermute x3, waiting for transfers between devices, shards(): out = out + lax.ppermute(own[dy], 'row', shift(0, dy, 0))  3.44 us
    unnamed x6, local copies, waits for them, and re-layouts  2.3 us
    ppermute x1, waiting for transfers between devices, shards(): held = keep + lax.ppermute(send, 'row', shift(0, 0, 1))  1.9 us
  transfers between devices with their start and end apart: 7, of which 6 were waited for; matrix products, arithmetic and copies ran while one was open for 0% of the time, Pallas kernels for 0%

profile of v1, /device:TPU:0, one launch (start us, length us, event | category | flops | bytes accessed | tf_op | source)
XLA Modules:
  0.0 38.2 jit_solution(10758879085400232487)
XLA Ops:
  0.0 0.0 copy-start
  0.0 0.9 %copy-done = s32[32768]{0:T(1024)S(1)} copy-done((s32[32768]{0:T(1024)S(1)}, s32[32768]{0:T(1024)}, u32[]{:S(2)}) %copy-start) | copy-done | bytes 131096
  0.9 0.0 copy-start.1
  0.9 0.7 %copy-done.1 = s32[2048]{0:T(1024)S(1)} copy-done((s32[2048]{0:T(1024)S(1)}, s32[2048]{0:T(1024)}, u32[]{:S(2)}) %copy-start.1) | copy-done | bytes 8216
  1.6 0.0 copy-start.2
  1.6 0.7 %copy-done.2 = s32[2048,1]{0,1:T(1,128)S(1)} copy-done((s32[2048,1]{0,1:T(1,128)S(1)}, s32[2048,1]{0,1:T(1,128)}, u32[]{:S(2)}) %copy-start.2) | copy-done | bytes 8216
  2.3 13.7 %shard_map.46 = (f32[16,64,128]{2,1,0:T(8,128)S(1)}, f32[16,64,128]{2,1,0:T(8,128)S(1)}) custom-call(f32[64,32768]{1,0:T(8,128)} %x_ref.1, s32[256,128]{1,0:T(8,128)S(1)} %bitcast.17, s32[16,128]{1,0:T(8,128)S(1)} %bitcast.18, s32[16,128]{1,0:T(8,128)S(1)} %bitcast.19), custom_call_target="tpu_custom_call" | custom-call | tf_op jit(solution)/shard_map/pallas_call | solution.py:174
  16.0 0.1 collective-permute-start
  16.1 1.9 %collective-permute-done = f32[16,64,128]{2,1,0:T(8,128)S(1)} collective-permute-done((f32[16,64,128]{2,1,0:T(8,128)S(1)}, f32[16,64,128]{2,1,0:T(8,128)S(1)}, u32[]{:S(2)}, u32[]{:S(2)}) %collective-permute-start) | collective-permute-done | bytes 524320 | tf_op jit(solution)/shard_map/ppermute | solution.py:214
  18.0 0.1 add.21
  18.1 1.6 %collective-permute-start.1 = (f32[4,64,128]{2,1,0:T(8,128)S(1)}, f32[4,64,128]{2,1,0:T(8,128)S(1)}, u32[]{:S(2)}, u32[]{:S(2)}) collective-permute-start(f32[4,64,128]{2,1,0:T(8,128)S(1)} %get-tuple-element.9), channel_id=1, source_target_pairs={{0,32},{4,36},{8,40},{12,44},{16,48},{20,52},{24,56},{28,60},{32,6... | collective-permute-start | bytes 393224 | tf_op jit(solution)/shard_map/ppermute | solution.py:217
  19.8 1.7 %collective-permute-start.3 = (f32[4,64,128]{2,1,0:T(8,128)S(1)}, f32[4,64,128]{2,1,0:T(8,128)S(1)}, u32[]{:S(2)}, u32[]{:S(2)}) collective-permute-start(f32[4,64,128]{2,1,0:T(8,128)S(1)} %get-tuple-element.10), channel_id=1, source_target_pairs={{0,96},{4,100},{8,104},{12,108},{16,112},{20,116},{24,120},{28,124... | collective-permute-start | bytes 393224 | tf_op jit(solution)/shard_map/ppermute | solution.py:217
  21.5 1.9 %collective-permute-start.2 = (f32[4,64,128]{2,1,0:T(8,128)S(1)}, f32[4,64,128]{2,1,0:T(8,128)S(1)}, u32[]{:S(2)}, u32[]{:S(2)}) collective-permute-start(f32[4,64,128]{2,1,0:T(8,128)S(1)} %get-tuple-element.11), channel_id=1, source_target_pairs={{0,64},{4,68},{8,72},{12,76},{16,80},{20,84},{24,88},{28,92},{32,9... | collective-permute-start | bytes 393224 | tf_op jit(solution)/shard_map/ppermute | solution.py:217
  23.4 1.6 %collective-permute-done.1 = f32[4,64,128]{2,1,0:T(8,128)S(1)} collective-permute-done((f32[4,64,128]{2,1,0:T(8,128)S(1)}, f32[4,64,128]{2,1,0:T(8,128)S(1)}, u32[]{:S(2)}, u32[]{:S(2)}) %collective-permute-start.1) | collective-permute-done | bytes 131104 | tf_op jit(solution)/shard_map/ppermute | solution.py:217
  25.0 1.1 %collective-permute-done.3 = f32[4,64,128]{2,1,0:T(8,128)S(1)} collective-permute-done((f32[4,64,128]{2,1,0:T(8,128)S(1)}, f32[4,64,128]{2,1,0:T(8,128)S(1)}, u32[]{:S(2)}, u32[]{:S(2)}) %collective-permute-start.3) | collective-permute-done | bytes 131104 | tf_op jit(solution)/shard_map/ppermute | solution.py:217
  26.0 2.8 %collective-permute-done.2 = f32[4,64,128]{2,1,0:T(8,128)S(1)} collective-permute-done((f32[4,64,128]{2,1,0:T(8,128)S(1)}, f32[4,64,128]{2,1,0:T(8,128)S(1)}, u32[]{:S(2)}, u32[]{:S(2)}) %collective-permute-start.2) | collective-permute-done | bytes 131104 | tf_op jit(solution)/shard_map/ppermute | solution.py:217
  28.9 1.6 %collective-permute-start.4 = (f32[64,128]{1,0:T(8,128)S(1)}, f32[64,128]{1,0:T(8,128)S(1)}, u32[]{:S(2)}, u32[]{:S(2)}) collective-permute-start(f32[64,128]{1,0:T(8,128)S(1)} %get-tuple-element.12), channel_id=1, source_target_pairs={{0,8},{4,12},{8,16},{12,20},{16,24},{20,28},{24,0},{28,4},{32,40},... | collective-permute-start | bytes 98312 | tf_op jit(solution)/shard_map/ppermute | solution.py:220
  30.5 1.7 %collective-permute-start.6 = (f32[64,128]{1,0:T(8,128)S(1)}, f32[64,128]{1,0:T(8,128)S(1)}, u32[]{:S(2)}, u32[]{:S(2)}) collective-permute-start(f32[64,128]{1,0:T(8,128)S(1)} %get-tuple-element.13), channel_id=1, source_target_pairs={{0,24},{4,28},{8,0},{12,4},{16,8},{20,12},{24,16},{28,20},{32,56},... | collective-permute-start | bytes 98312 | tf_op jit(solution)/shard_map/ppermute | solution.py:220
  32.2 2.0 %collective-permute-start.5 = (f32[64,128]{1,0:T(8,128)S(1)}, f32[64,128]{1,0:T(8,128)S(1)}, u32[]{:S(2)}, u32[]{:S(2)}) collective-permute-start(f32[64,128]{1,0:T(8,128)S(1)} %get-tuple-element.14), channel_id=1, source_target_pairs={{0,16},{4,20},{8,24},{12,28},{16,0},{20,4},{24,8},{28,12},{32,48},... | collective-permute-start | bytes 98312 | tf_op jit(solution)/shard_map/ppermute | solution.py:220
  34.2 0.0 collective-permute-done.4
  34.2 0.5 %collective-permute-done.6 = f32[64,128]{1,0:T(8,128)S(1)} collective-permute-done((f32[64,128]{1,0:T(8,128)S(1)}, f32[64,128]{1,0:T(8,128)S(1)}, u32[]{:S(2)}, u32[]{:S(2)}) %collective-permute-start.6) | collective-permute-done | bytes 32800 | tf_op jit(solution)/shard_map/ppermute | solution.py:220
  34.7 2.9 %collective-permute-done.5 = f32[64,128]{1,0:T(8,128)S(1)} collective-permute-done((f32[64,128]{1,0:T(8,128)S(1)}, f32[64,128]{1,0:T(8,128)S(1)}, u32[]{:S(2)}, u32[]{:S(2)}) %collective-permute-start.5) | collective-permute-done | bytes 32800 | tf_op jit(solution)/shard_map/ppermute | solution.py:220
  37.6 0.6 %fusion.4 = f32[64,128]{1,0:T(8,128)} fusion(f32[64,128]{1,0:T(8,128)S(1)} %collective-permute-done.6, f32[64,128]{1,0:T(8,128)S(1)} %collective-permute-done.5, f32[64,128]{1,0:T(8,128)S(1)} %collective-permute-done.4, f32[4,64,128]{2,1,0:T(8,128)S(1)} %fusion.1), kind=kLoop, calls=%fused_computation.9 | loop fusion | flops 24576 | bytes 163840 | tf_op jit(solution)/shard_map/add | solution.py:220
  (3 shorter events, 0.1 us)
Async XLA Ops:
  0.0 0.9 %copy-start = (s32[32768]{0:T(1024)S(1)}, s32[32768]{0:T(1024)}, u32[]{:S(2)}) copy-start(s32[32768]{0:T(1024)} %param.5) | copy-start | bytes 393220
  0.9 0.7 %copy-start.1 = (s32[2048]{0:T(1024)S(1)}, s32[2048]{0:T(1024)}, u32[]{:S(2)}) copy-start(s32[2048]{0:T(1024)} %param.6) | copy-start | bytes 24580
  1.6 0.7 %copy-start.2 = (s32[2048,1]{0,1:T(1,128)S(1)}, s32[2048,1]{0,1:T(1,128)}, u32[]{:S(2)}) copy-start(s32[2048,1]{0,1:T(1,128)} %param.7) | copy-start | bytes 24580
  16.0 2.0 %collective-permute-start = (f32[16,64,128]{2,1,0:T(8,128)S(1)}, f32[16,64,128]{2,1,0:T(8,128)S(1)}, u32[]{:S(2)}, u32[]{:S(2)}) collective-permute-start(f32[16,64,128]{2,1,0:T(8,128)S(1)} %get-tuple-element.8), channel_id=1, source_target_pairs={{0,4},{4,0},{8,12},{12,8},{16,20},{20,16},{24,28},{28,24},{32,36},... | collective-permute-start | bytes 1572872 | tf_op jit(solution)/shard_map/ppermute | solution.py:214
  18.1 6.8 %collective-permute-start.1 = (f32[4,64,128]{2,1,0:T(8,128)S(1)}, f32[4,64,128]{2,1,0:T(8,128)S(1)}, u32[]{:S(2)}, u32[]{:S(2)}) collective-permute-start(f32[4,64,128]{2,1,0:T(8,128)S(1)} %get-tuple-element.9), channel_id=1, source_target_pairs={{0,32},{4,36},{8,40},{12,44},{16,48},{20,52},{24,56},{28,60},{32,6... | collective-permute-start | bytes 393224 | tf_op jit(solution)/shard_map/ppermute | solution.py:217
  19.8 6.3 %collective-permute-start.3 = (f32[4,64,128]{2,1,0:T(8,128)S(1)}, f32[4,64,128]{2,1,0:T(8,128)S(1)}, u32[]{:S(2)}, u32[]{:S(2)}) collective-permute-start(f32[4,64,128]{2,1,0:T(8,128)S(1)} %get-tuple-element.10), channel_id=1, source_target_pairs={{0,96},{4,100},{8,104},{12,108},{16,112},{20,116},{24,120},{28,124... | collective-permute-start | bytes 393224 | tf_op jit(solution)/shard_map/ppermute | solution.py:217
  21.5 7.4 %collective-permute-start.2 = (f32[4,64,128]{2,1,0:T(8,128)S(1)}, f32[4,64,128]{2,1,0:T(8,128)S(1)}, u32[]{:S(2)}, u32[]{:S(2)}) collective-permute-start(f32[4,64,128]{2,1,0:T(8,128)S(1)} %get-tuple-element.11), channel_id=1, source_target_pairs={{0,64},{4,68},{8,72},{12,76},{16,80},{20,84},{24,88},{28,92},{32,9... | collective-permute-start | bytes 393224 | tf_op jit(solution)/shard_map/ppermute | solution.py:217
  28.9 5.3 %collective-permute-start.4 = (f32[64,128]{1,0:T(8,128)S(1)}, f32[64,128]{1,0:T(8,128)S(1)}, u32[]{:S(2)}, u32[]{:S(2)}) collective-permute-start(f32[64,128]{1,0:T(8,128)S(1)} %get-tuple-element.12), channel_id=1, source_target_pairs={{0,8},{4,12},{8,16},{12,20},{16,24},{20,28},{24,0},{28,4},{32,40},... | collective-permute-start | bytes 98312 | tf_op jit(solution)/shard_map/ppermute | solution.py:220
  30.5 4.2 %collective-permute-start.6 = (f32[64,128]{1,0:T(8,128)S(1)}, f32[64,128]{1,0:T(8,128)S(1)}, u32[]{:S(2)}, u32[]{:S(2)}) collective-permute-start(f32[64,128]{1,0:T(8,128)S(1)} %get-tuple-element.13), channel_id=1, source_target_pairs={{0,24},{4,28},{8,0},{12,4},{16,8},{20,12},{24,16},{28,20},{32,56},... | collective-permute-start | bytes 98312 | tf_op jit(solution)/shard_map/ppermute | solution.py:220
  32.2 5.4 %collective-permute-start.5 = (f32[64,128]{1,0:T(8,128)S(1)}, f32[64,128]{1,0:T(8,128)S(1)}, u32[]{:S(2)}, u32[]{:S(2)}) collective-permute-start(f32[64,128]{1,0:T(8,128)S(1)} %get-tuple-element.14), channel_id=1, source_target_pairs={{0,16},{4,20},{8,24},{12,28},{16,0},{20,4},{24,8},{28,12},{32,48},... | collective-permute-start | bytes 98312 | tf_op jit(solution)/shard_map/ppermute | solution.py:220

commit v2 on v1

v2 whole, which is shorter than its diff:
```python
import functools

import jax
import jax.numpy as jnp
from jax import lax
from jax.experimental import pallas as pl
from jax.experimental.pallas import tpu as pltpu
from jax.sharding import PartitionSpec as P

LANES = 128
SIDE_X, SIDE_Y = 4, 4
CHUNKS = 8
INNER = 16
DEPTH = 256
CAPACITY = 128
BLOCKS = 32


def parity(value, bits):
    shift = 1
    while shift < bits:
        value = value ^ (value >> shift)
        shift = shift * 2
    return value & 1


def butterflies(values):
    half = 1
    values = list(values)
    while half < len(values):
        for start in range(0, len(values), 2 * half):
            for at in range(start, start + half):
                first, second = values[at], values[at + half]
                values[at], values[at + half] = first + second, first - second
        half = half * 2
    return values


def list_samples(me, picks, owners, rows_here, listed_ref, weight_ref):
    core, along_y, along_x = me & 1, (me >> 1) & 3, me >> 3
    owner_core = owners & 1
    rel_x = ((owners >> 3) - along_x) & 3
    rel_y = ((owners >> 1) - along_y) & 3
    first = jnp.where(owner_core == 0, rel_x, rel_y)
    second = jnp.where(owner_core == 0, rel_y, rel_x)
    rel = ((owner_core ^ core) << 4) | (first << 2) | second
    source = picks // rows_here
    offset = picks % rows_here
    sign = (1 - 2 * parity(source & me, 8)).astype(jnp.float32)
    column = offset // DEPTH
    odd = (column & 1).astype(jnp.float32)
    row = (column >> 1) * DEPTH + (offset % DEPTH)
    pieces = [
        sign * (1.0 - odd),
        sign * odd,
        (row & 127).astype(jnp.float32),
        (row >> 7).astype(jnp.float32),
    ]
    groups = picks.shape[0]
    up = lax.broadcasted_iota(jnp.int32, (LANES, 2 * LANES), 0)
    to = lax.broadcasted_iota(jnp.int32, (LANES, 2 * LANES), 1)
    upper = jnp.where((to >= LANES) | (up < to), 1.0, 0.0).astype(jnp.bfloat16)
    target = lax.broadcasted_iota(jnp.int32, (BLOCKS, LANES), 0)
    place = lax.broadcasted_iota(jnp.int32, (CAPACITY, LANES), 0)
    onehot = [jnp.where(rel[g:g + 1] == target, 1.0, 0.0) for g in range(groups)]
    counted = jnp.dot(
        jnp.concatenate(onehot, axis=0).astype(jnp.bfloat16),
        upper,
        preferred_element_type=jnp.float32,
    )
    base = jnp.zeros((BLOCKS, LANES), jnp.float32)
    total = jnp.zeros((len(pieces) * BLOCKS, LANES), jnp.float32)
    for g in range(groups):
        here = counted[g * BLOCKS:(g + 1) * BLOCKS]
        rank = jnp.sum(onehot[g] * (here[:, :LANES] + base), axis=0, keepdims=True)
        base = base + here[:, LANES:]
        at = jnp.where(rank.astype(jnp.int32) == place, 1.0, 0.0).astype(jnp.bfloat16)
        held = [onehot[g] * piece[g:g + 1] for piece in pieces]
        total = total + lax.dot_general(
            jnp.concatenate(held, axis=0).astype(jnp.bfloat16), at,
            (((1,), (1,)), ((), ())), preferred_element_type=jnp.float32,
        )
    weight_ref[...] = total[:2 * BLOCKS] * jnp.float32(2.0 ** -10)
    low = total[2 * BLOCKS:3 * BLOCKS].astype(jnp.int32)
    high = total[3 * BLOCKS:].astype(jnp.int32)
    listed_ref[...] = (base.astype(jnp.int32) << 16) | (high << 7) | low


def take_rows(first, blocks, table, listed, rows):
    @pl.loop(0, blocks)
    def _(b):
        count = listed[first + b, 0] >> 16

        @pl.loop(0, (count + 7) >> 3)
        def _(eight):
            for i in range(8):
                at = eight * 8 + i
                row = listed[first + b, at] & 16383
                rows[pl.ds(b * CAPACITY + at, 1), :] = table[pl.ds(row, 1), :]


def turn_rows(first, blocks, rows, weight, out_ref):
    width = out_ref.shape[1]

    @pl.loop(0, blocks // 2)
    def _(pair):
        for b in (2 * pair, 2 * pair + 1):
            turned = rows[pl.ds(b * CAPACITY, CAPACITY), :].T
            even = weight[pl.ds(first + b, 1), :]
            odd = weight[pl.ds(BLOCKS + first + b, 1), :]
            zero = jnp.zeros((width, CAPACITY), jnp.float32)
            value = jnp.where(even != 0.0, turned[:width] * even, zero)
            out_ref[b] = jnp.where(odd != 0.0, turned[width:] * odd, value)


def transform_kernel(
    x_ref, bits_ref, picks_ref, owners_ref, send_ref, table, listed_ref, weight,
    x_buf, bits, picks, owners, signs, had, parts_a, parts_b, listed, rows,
    x_sem, small_sem, l_sem,
):
    width = x_ref.shape[0]
    rows_here = x_ref.shape[1]
    span = rows_here // CHUNKS
    me = lax.axis_index("row")

    small = [
        pltpu.make_async_copy(source, to, small_sem.at[n])
        for n, (source, to) in enumerate(
            ((picks_ref, picks), (owners_ref, owners), (bits_ref, bits))
        )
    ]
    chunks = [
        pltpu.make_async_copy(
            x_ref.at[:, g * span:(g + 1) * span], x_buf.at[g], x_sem.at[g]
        )
        for g in range(CHUNKS)
    ]
    for copy in small + chunks:
        copy.start()

    i = lax.broadcasted_iota(jnp.int32, (DEPTH, DEPTH), 0)
    k = lax.broadcasted_iota(jnp.int32, (DEPTH, DEPTH), 1)
    matrix = (1 - 2 * parity(i & k, 8)).astype(jnp.float32).astype(jnp.bfloat16)
    had[:, :DEPTH] = matrix
    had[:, DEPTH:] = matrix
    small[0].wait()
    small[1].wait()
    list_samples(me, picks[...], owners[...], rows_here, listed_ref, weight)
    listing = pltpu.make_async_copy(listed_ref, listed, l_sem)
    listing.start()
    small[2].wait()
    signs[...] = (1 - 2 * bits[...]).astype(jnp.float32)

    def prepare(g, it, parts):
        c = it * 16
        for half in range(2):
            values = []
            for j in range(INNER):
                at = j * DEPTH + half * LANES
                line = (g * span + at) // LANES
                values.append(
                    x_buf[g, pl.ds(c, 16), at:at + LANES] * signs[line:line + 1, :]
                )
            for j, value in enumerate(butterflies(values)):
                high = value.astype(jnp.bfloat16)
                low = (value - high.astype(jnp.float32)).astype(jnp.bfloat16)
                at = pl.ds(j * width + c, 16)
                parts[at, half * LANES:(half + 1) * LANES] = high
                parts[at, DEPTH + half * LANES:DEPTH + (half + 1) * LANES] = low

    def multiply(g, it, parts):
        made = lax.dot_general(
            had[...], parts[pl.ds(it * 4 * width, 4 * width), :],
            (((1,), (1,)), ((), ())), preferred_element_type=jnp.float32,
        )
        at = (g * (INNER // 2) + it * 2) * DEPTH
        table[pl.ds(at, DEPTH), :] = made[:, :LANES]
        table[pl.ds(at + DEPTH, DEPTH), :] = made[:, LANES:]

    both = (parts_a, parts_b)
    for g in range(CHUNKS + 1):
        if g < CHUNKS:
            chunks[g].wait()

        @pl.loop(0, 4)
        def _(it):
            if g > 0:
                multiply(g - 1, it, both[(g - 1) % 2])
            if g < CHUNKS:
                prepare(g, it, both[g % 2])

    stretch = table.shape[0] // CHUNKS
    step = 32

    @pl.loop(0, stretch // step)
    def _(at):
        values = [table[pl.ds(g * stretch + at * step, step), :] for g in range(CHUNKS)]
        for g, value in enumerate(butterflies(values)):
            table[pl.ds(g * stretch + at * step, step), :] = value

    listing.wait()
    take_rows(BLOCKS // 2, BLOCKS // 2, table, listed, rows)
    turn_rows(BLOCKS // 2, BLOCKS // 2, rows, weight, send_ref)


def take_kernel(first, table, listed_ref, weight, out_ref, listed, rows, l_sem):
    listing = pltpu.make_async_copy(listed_ref, listed, l_sem)
    listing.start()
    listing.wait()
    blocks = out_ref.shape[0]
    take_rows(first, blocks, table, listed, rows)
    turn_rows(first, blocks, rows, weight, out_ref)


VMEM = pl.BlockSpec(memory_space=pltpu.VMEM)
ANY = pl.BlockSpec(memory_space=pltpu.HBM)


def transform(design, bits, picks, owners):
    width, rows_here = design.shape
    f32, i32 = jnp.float32, jnp.int32
    return pl.pallas_call(
        transform_kernel,
        out_shape=(
            jax.ShapeDtypeStruct((BLOCKS // 2, width, CAPACITY), f32),
            jax.ShapeDtypeStruct((rows_here // 2, LANES), f32),
            jax.ShapeDtypeStruct((BLOCKS, LANES), i32),
            jax.ShapeDtypeStruct((2 * BLOCKS, LANES), f32),
        ),
        in_specs=[ANY] * 4,
        out_specs=(VMEM,) * 4,
        scratch_shapes=[
            pltpu.VMEM((CHUNKS, width, rows_here // CHUNKS), f32),
            pltpu.VMEM(bits.shape, i32),
            pltpu.VMEM(picks.shape, i32),
            pltpu.VMEM(owners.shape, i32),
            pltpu.VMEM(bits.shape, f32),
            pltpu.VMEM((DEPTH, 2 * DEPTH), jnp.bfloat16),
            pltpu.VMEM((INNER * width, 2 * DEPTH), jnp.bfloat16),
            pltpu.VMEM((INNER * width, 2 * DEPTH), jnp.bfloat16),
            pltpu.SMEM((BLOCKS, LANES), i32),
            pltpu.VMEM((BLOCKS // 2 * CAPACITY, LANES), f32),
            pltpu.SemaphoreType.DMA((CHUNKS,)),
            pltpu.SemaphoreType.DMA((3,)),
            pltpu.SemaphoreType.DMA,
        ],
        compiler_params=pltpu.CompilerParams(vmem_limit_bytes=24 << 20),
    )(*[
        pltpu.with_memory_space_constraint(a, pltpu.HBM)
        for a in (design, bits, picks, owners)
    ])


def take(first, blocks, width, table, listed, weight):
    return pl.pallas_call(
        functools.partial(take_kernel, first),
        out_shape=jax.ShapeDtypeStruct((blocks, width, CAPACITY), jnp.float32),
        in_specs=[VMEM] * 3,
        out_specs=VMEM,
        scratch_shapes=[
            pltpu.SMEM((BLOCKS, LANES), jnp.int32),
            pltpu.VMEM((blocks * CAPACITY, LANES), jnp.float32),
            pltpu.SemaphoreType.DMA,
        ],
        compiler_params=pltpu.CompilerParams(vmem_limit_bytes=24 << 20),
        cost_estimate=pl.CostEstimate(
            flops=0, bytes_accessed=blocks << 18, transcendentals=0
        ),
    )(table, listed, weight)


def place(x, y, core):
    return (x * SIDE_Y + y) * 2 + core


def core_swap():
    return [(i, i ^ 1) for i in range(BLOCKS)]


def shift(step, first):
    pairs = []
    for x in range(SIDE_X):
        for y in range(SIDE_Y):
            for core in range(2):
                if (core == 0) == first:
                    to = place((x + step) % SIDE_X, y, core)
                else:
                    to = place(x, (y + step) % SIDE_Y, core)
                pairs.append((place(x, y, core), to))
    return pairs


def shards(design, sign_bits, picks, owners):
    width = design.shape[0]
    send, *made = transform(
        design,
        sign_bits.reshape(-1, LANES),
        picks.reshape(-1, LANES),
        owners.reshape(-1, LANES),
    )
    held = lax.ppermute(send, "row", core_swap())
    held = take(0, BLOCKS // 2, width, *made) + held
    own = held[0:4]
    for step in (1, 2, 3):
        own = own + lax.ppermute(held[step * 4:step * 4 + 4], "row", shift(step, True))
    out = own[0]
    for step in (1, 2, 3):
        out = out + lax.ppermute(own[step], "row", shift(step, False))
    return out


def solution(mesh):
    placed = (P("col", "row"), P("row"), P(), P())
    return jax.shard_map(
        shards, mesh=mesh, in_specs=placed, out_specs=P("col", "row"), check_vma=False
    )
```

time: 38.4 us -> 42.8 us (1.11)
  Pallas kernels: 13.7 us -> 23 us
  waiting for transfers between devices: 10.8 us -> 7.94 us
  local copies, waits for them, and re-layouts: 2.33 us -> 0.04 us
    pallas_call x1 -> x2, Pallas kernels: 13.7 us -> 23 us  [the longest x1 18.3 us: transform(): pl.pallas_call(transform_kernel, out_shape=(jax.ShapeDtypeStruct((BLOCKS...]
    ppermute x7, waiting for transfers between devices: 10.8 us -> 7.94 us  [the longest x3 4.58 us: shards(): lax.ppermute(held[step * 4:step * 4 + 4], 'row', shift(step, True))]
    unnamed x6 -> x0, local copies, waits for them, and re-layouts: 2.3 us -> none
  transfers between devices with their start and end apart: 7 -> 7, of which waited for: 6 -> 5; matrix products, arithmetic and copies ran while one was open for 0% -> 0% of each run, Pallas kernels for 0% -> 11%
where the time goes in v2:
time: 42.8 us; the launch traced here: 42.4 us
  Pallas kernels  23 us (54%)
  starting transfers between devices  10.7 us (25%)
  waiting for transfers between devices  7.94 us (19%)
  other arithmetic  0.71 us (2%)
    pallas_call x1, Pallas kernels, transform(): pl.pallas_call(transform_kernel, out_shape=(jax.ShapeDtypeStruct((BLOCKS...  18.3 us
    ppermute x3, starting transfers between devices, shards(): out = out + lax.ppermute(own[step], 'row', shift(step, False))  5.37 us
    ppermute x3, starting transfers between devices, shards(): lax.ppermute(held[step * 4:step * 4 + 4], 'row', shift(step, True))  5.2 us
    pallas_call x1, Pallas kernels, take(): pl.pallas_call(functools.partial(take_kernel, first), out_shape=jax.Shape...  4.66 us
    ppermute x3, waiting for transfers between devices, shards(): lax.ppermute(held[step * 4:step * 4 + 4], 'row', shift(step, True))  4.58 us
    ppermute x3, waiting for transfers between devices, shards(): out = out + lax.ppermute(own[step], 'row', shift(step, False))  3.36 us
  transfers between devices with their start and end apart: 7, of which 5 were waited for; matrix products, arithmetic and copies ran while one was open for 0% of the time, Pallas kernels for 11%

profile of v2, /device:TPU:0, one launch (start us, length us, event | category | flops | bytes accessed | tf_op | source)
XLA Modules:
  0.0 42.4 jit_solution(4267673030460672166)
XLA Ops:
  0.0 18.3 %shard_map.46 = (f32[16,64,128]{2,1,0:T(8,128)S(1)}, f32[16384,128]{1,0:T(8,128)S(1)}, s32[32,128]{1,0:T(8,128)S(1)}, f32[64,128]{1,0:T(8,128)S(1)}) custom-call(f32[64,32768]{1,0:T(8,128)} %x_ref.1, s32[256,128]{1,0:T(8,128)} %bitcast.17, s32[16,128]{1,0:T(8,128)} %bitcast.18, s32[16,128]{1,0:T(8,128)} %bitcast.19), custom_call_target="tpu_custom_call" | custom-call | tf_op jit(solution)/shard_map/pallas_call | solution.py:222
  18.3 0.1 collective-permute-start
  18.4 4.7 %shard_map.47 = f32[16,64,128]{2,1,0:T(8,128)S(1)} custom-call(f32[16384,128]{1,0:T(8,128)S(1)} %get-tuple-element.9.table, s32[32,128]{1,0:T(8,128)S(1)} %get-tuple-element.10.listed_ref, f32[64,128]{1,0:T(8,128)S(1)} %get-tuple-element.11.weight), custom_call_target="tpu_custom_call" | custom-call | bytes 4194304 | tf_op jit(solution)/shard_map/pallas_call | solution.py:255
  23.1 0.0 collective-permute-done
  23.1 0.1 add.21
  23.2 1.6 %collective-permute-start.1 = (f32[4,64,128]{2,1,0:T(8,128)S(1)}, f32[4,64,128]{2,1,0:T(8,128)S(1)}, u32[]{:S(2)}, u32[]{:S(2)}) collective-permute-start(f32[4,64,128]{2,1,0:T(8,128)S(1)} %get-tuple-element.13), channel_id=1, source_target_pairs={{0,32},{4,12},{8,40},{12,20},{16,48},{20,28},{24,56},{28,4},{32,64... | collective-permute-start | bytes 393224 | tf_op jit(solution)/shard_map/ppermute | solution.py:305
  24.9 1.7 %collective-permute-start.3 = (f32[4,64,128]{2,1,0:T(8,128)S(1)}, f32[4,64,128]{2,1,0:T(8,128)S(1)}, u32[]{:S(2)}, u32[]{:S(2)}) collective-permute-start(f32[4,64,128]{2,1,0:T(8,128)S(1)} %get-tuple-element.14), channel_id=1, source_target_pairs={{0,96},{4,28},{8,104},{12,4},{16,112},{20,12},{24,120},{28,20},{32... | collective-permute-start | bytes 393224 | tf_op jit(solution)/shard_map/ppermute | solution.py:305
  26.5 1.9 %collective-permute-start.2 = (f32[4,64,128]{2,1,0:T(8,128)S(1)}, f32[4,64,128]{2,1,0:T(8,128)S(1)}, u32[]{:S(2)}, u32[]{:S(2)}) collective-permute-start(f32[4,64,128]{2,1,0:T(8,128)S(1)} %get-tuple-element.15), channel_id=1, source_target_pairs={{0,64},{4,20},{8,72},{12,28},{16,80},{20,4},{24,88},{28,12},{32,96... | collective-permute-start | bytes 393224 | tf_op jit(solution)/shard_map/ppermute | solution.py:305
  28.4 1.0 %collective-permute-done.1 = f32[4,64,128]{2,1,0:T(8,128)S(1)} collective-permute-done((f32[4,64,128]{2,1,0:T(8,128)S(1)}, f32[4,64,128]{2,1,0:T(8,128)S(1)}, u32[]{:S(2)}, u32[]{:S(2)}) %collective-permute-start.1) | collective-permute-done | bytes 131104 | tf_op jit(solution)/shard_map/ppermute | solution.py:305
  29.5 0.4 collective-permute-done.3
  29.8 3.2 %collective-permute-done.2 = f32[4,64,128]{2,1,0:T(8,128)S(1)} collective-permute-done((f32[4,64,128]{2,1,0:T(8,128)S(1)}, f32[4,64,128]{2,1,0:T(8,128)S(1)}, u32[]{:S(2)}, u32[]{:S(2)}) %collective-permute-start.2) | collective-permute-done | bytes 131104 | tf_op jit(solution)/shard_map/ppermute | solution.py:305
  33.0 1.7 %collective-permute-start.4 = (f32[64,128]{1,0:T(8,128)S(1)}, f32[64,128]{1,0:T(8,128)S(1)}, u32[]{:S(2)}, u32[]{:S(2)}) collective-permute-start(f32[64,128]{1,0:T(8,128)S(1)} %get-tuple-element.16), channel_id=1, source_target_pairs={{0,8},{4,36},{8,16},{12,44},{16,24},{20,52},{24,0},{28,60},{32,40}... | collective-permute-start | bytes 98312 | tf_op jit(solution)/shard_map/ppermute | solution.py:308
  34.8 1.6 %collective-permute-start.6 = (f32[64,128]{1,0:T(8,128)S(1)}, f32[64,128]{1,0:T(8,128)S(1)}, u32[]{:S(2)}, u32[]{:S(2)}) collective-permute-start(f32[64,128]{1,0:T(8,128)S(1)} %get-tuple-element.17), channel_id=1, source_target_pairs={{0,24},{4,100},{8,0},{12,108},{16,8},{20,116},{24,16},{28,124},{32... | collective-permute-start | bytes 98312 | tf_op jit(solution)/shard_map/ppermute | solution.py:308
  36.3 2.1 %collective-permute-start.5 = (f32[64,128]{1,0:T(8,128)S(1)}, f32[64,128]{1,0:T(8,128)S(1)}, u32[]{:S(2)}, u32[]{:S(2)}) collective-permute-start(f32[64,128]{1,0:T(8,128)S(1)} %get-tuple-element.18), channel_id=1, source_target_pairs={{0,16},{4,68},{8,24},{12,76},{16,0},{20,84},{24,8},{28,92},{32,48}... | collective-permute-start | bytes 98312 | tf_op jit(solution)/shard_map/ppermute | solution.py:308
  38.4 0.0 collective-permute-done.4
  38.4 0.3 collective-permute-done.6
  38.7 3.1 %collective-permute-done.5 = f32[64,128]{1,0:T(8,128)S(1)} collective-permute-done((f32[64,128]{1,0:T(8,128)S(1)}, f32[64,128]{1,0:T(8,128)S(1)}, u32[]{:S(2)}, u32[]{:S(2)}) %collective-permute-start.5) | collective-permute-done | bytes 32800 | tf_op jit(solution)/shard_map/ppermute | solution.py:308
  41.8 0.6 %fusion.4 = f32[64,128]{1,0:T(8,128)} fusion(f32[64,128]{1,0:T(8,128)S(1)} %collective-permute-done.6, f32[64,128]{1,0:T(8,128)S(1)} %collective-permute-done.5, f32[64,128]{1,0:T(8,128)S(1)} %collective-permute-done.4, f32[4,64,128]{2,1,0:T(8,128)S(1)} %fusion.1), kind=kLoop, calls=%fused_computation.9 | loop fusion | flops 24576 | bytes 163840 | tf_op jit(solution)/shard_map/add | solution.py:308
  (3 shorter events, 0.1 us)
Async XLA Ops:
  18.3 4.8 %collective-permute-start = (f32[16,64,128]{2,1,0:T(8,128)S(1)}, f32[16,64,128]{2,1,0:T(8,128)S(1)}, u32[]{:S(2)}, u32[]{:S(2)}) collective-permute-start(f32[16,64,128]{2,1,0:T(8,128)S(1)} %get-tuple-element.12), channel_id=1, source_target_pairs={{0,4},{4,0},{8,12},{12,8},{16,20},{20,16},{24,28},{28,24},{32,36},... | collective-permute-start | bytes 1572872 | tf_op jit(solution)/shard_map/ppermute | solution.py:301
  23.2 6.2 %collective-permute-start.1 = (f32[4,64,128]{2,1,0:T(8,128)S(1)}, f32[4,64,128]{2,1,0:T(8,128)S(1)}, u32[]{:S(2)}, u32[]{:S(2)}) collective-permute-start(f32[4,64,128]{2,1,0:T(8,128)S(1)} %get-tuple-element.13), channel_id=1, source_target_pairs={{0,32},{4,12},{8,40},{12,20},{16,48},{20,28},{24,56},{28,4},{32,64... | collective-permute-start | bytes 393224 | tf_op jit(solution)/shard_map/ppermute | solution.py:305
  24.9 5.0 %collective-permute-start.3 = (f32[4,64,128]{2,1,0:T(8,128)S(1)}, f32[4,64,128]{2,1,0:T(8,128)S(1)}, u32[]{:S(2)}, u32[]{:S(2)}) collective-permute-start(f32[4,64,128]{2,1,0:T(8,128)S(1)} %get-tuple-element.14), channel_id=1, source_target_pairs={{0,96},{4,28},{8,104},{12,4},{16,112},{20,12},{24,120},{28,20},{32... | collective-permute-start | bytes 393224 | tf_op jit(solution)/shard_map/ppermute | solution.py:305
  26.5 6.5 %collective-permute-start.2 = (f32[4,64,128]{2,1,0:T(8,128)S(1)}, f32[4,64,128]{2,1,0:T(8,128)S(1)}, u32[]{:S(2)}, u32[]{:S(2)}) collective-permute-start(f32[4,64,128]{2,1,0:T(8,128)S(1)} %get-tuple-element.15), channel_id=1, source_target_pairs={{0,64},{4,20},{8,72},{12,28},{16,80},{20,4},{24,88},{28,12},{32,96... | collective-permute-start | bytes 393224 | tf_op jit(solution)/shard_map/ppermute | solution.py:305
  33.0 5.4 %collective-permute-start.4 = (f32[64,128]{1,0:T(8,128)S(1)}, f32[64,128]{1,0:T(8,128)S(1)}, u32[]{:S(2)}, u32[]{:S(2)}) collective-permute-start(f32[64,128]{1,0:T(8,128)S(1)} %get-tuple-element.16), channel_id=1, source_target_pairs={{0,8},{4,36},{8,16},{12,44},{16,24},{20,52},{24,0},{28,60},{32,40}... | collective-permute-start | bytes 98312 | tf_op jit(solution)/shard_map/ppermute | solution.py:308
  34.8 3.9 %collective-permute-start.6 = (f32[64,128]{1,0:T(8,128)S(1)}, f32[64,128]{1,0:T(8,128)S(1)}, u32[]{:S(2)}, u32[]{:S(2)}) collective-permute-start(f32[64,128]{1,0:T(8,128)S(1)} %get-tuple-element.17), channel_id=1, source_target_pairs={{0,24},{4,100},{8,0},{12,108},{16,8},{20,116},{24,16},{28,124},{32... | collective-permute-start | bytes 98312 | tf_op jit(solution)/shard_map/ppermute | solution.py:308
  36.3 5.4 %collective-permute-start.5 = (f32[64,128]{1,0:T(8,128)S(1)}, f32[64,128]{1,0:T(8,128)S(1)}, u32[]{:S(2)}, u32[]{:S(2)}) collective-permute-start(f32[64,128]{1,0:T(8,128)S(1)} %get-tuple-element.18), channel_id=1, source_target_pairs={{0,16},{4,68},{8,24},{12,76},{16,0},{20,84},{24,8},{28,92},{32,48}... | collective-permute-start | bytes 98312 | tf_op jit(solution)/shard_map/ppermute | solution.py:308

commit v3 on v2

--- a/solution.py
+++ b/solution.py
@@ -13,6 +13,8 @@
 INNER = 16
 DEPTH = 256
 CAPACITY = 128
+STEP = 32
+AHEAD = 3
 BLOCKS = 32
 
 
@@ -83,20 +85,20 @@
     weight_ref[...] = total[:2 * BLOCKS] * jnp.float32(2.0 ** -10)
     low = total[2 * BLOCKS:3 * BLOCKS].astype(jnp.int32)
     high = total[3 * BLOCKS:].astype(jnp.int32)
-    listed_ref[...] = (base.astype(jnp.int32) << 16) | (high << 7) | low
+    listed_ref[:BLOCKS] = (high << 7) | low
+    listed_ref[BLOCKS:] = base.astype(jnp.int32)
 
 
 def take_rows(first, blocks, table, listed, rows):
     @pl.loop(0, blocks)
     def _(b):
-        count = listed[first + b, 0] >> 16
-
-        @pl.loop(0, (count + 7) >> 3)
-        def _(eight):
-            for i in range(8):
-                at = eight * 8 + i
-                row = listed[first + b, at] & 16383
-                rows[pl.ds(b * CAPACITY + at, 1), :] = table[pl.ds(row, 1), :]
+        count = listed[BLOCKS + first + b, 0]
+        for start in range(0, CAPACITY, STEP):
+            @pl.when(count > start)
+            def _():
+                for at in range(start, start + STEP):
+                    row = listed[first + b, at]
+                    rows[pl.ds(b * CAPACITY + at, 1), :] = table[pl.ds(row, 1), :]
 
 
 def turn_rows(first, blocks, rows, weight, out_ref):
@@ -129,14 +131,16 @@
             ((picks_ref, picks), (owners_ref, owners), (bits_ref, bits))
         )
     ]
-    chunks = [
-        pltpu.make_async_copy(
-            x_ref.at[:, g * span:(g + 1) * span], x_buf.at[g], x_sem.at[g]
+    def chunk(g):
+        at = pl.multiple_of(g * span, span)
+        return pltpu.make_async_copy(
+            x_ref.at[:, pl.ds(at, span)], x_buf.at[g], x_sem.at[g]
         )
-        for g in range(CHUNKS)
-    ]
-    for copy in small + chunks:
+
+    for copy in small:
         copy.start()
+    for g in range(AHEAD):
+        chunk(g).start()
 
     i = lax.broadcasted_iota(jnp.int32, (DEPTH, DEPTH), 0)
     k = lax.broadcasted_iota(jnp.int32, (DEPTH, DEPTH), 1)
@@ -151,43 +155,63 @@
     small[2].wait()
     signs[...] = (1 - 2 * bits[...]).astype(jnp.float32)
 
-    def prepare(g, it, parts):
-        c = it * 16
-        for half in range(2):
-            values = []
-            for j in range(INNER):
-                at = j * DEPTH + half * LANES
-                line = (g * span + at) // LANES
-                values.append(
-                    x_buf[g, pl.ds(c, 16), at:at + LANES] * signs[line:line + 1, :]
-                )
-            for j, value in enumerate(butterflies(values)):
-                high = value.astype(jnp.bfloat16)
-                low = (value - high.astype(jnp.float32)).astype(jnp.bfloat16)
-                at = pl.ds(j * width + c, 16)
-                parts[at, half * LANES:(half + 1) * LANES] = high
-                parts[at, DEPTH + half * LANES:DEPTH + (half + 1) * LANES] = low
-
-    def multiply(g, it, parts):
+    def prepare(g, c, half, parts):
+        values = []
+        for j in range(INNER):
+            at = j * DEPTH + half * LANES
+            sign = signs[pl.ds(g * (span // LANES) + at // LANES, 1), :]
+            values.append(x_buf[g, c:c + 16, at:at + LANES] * sign)
+        for j, value in enumerate(butterflies(values)):
+            high = value.astype(jnp.bfloat16)
+            low = (value - high.astype(jnp.float32)).astype(jnp.bfloat16)
+            at = slice(j * width + c, j * width + c + 16)
+            parts[at, half * LANES:(half + 1) * LANES] = high
+            parts[at, DEPTH + half * LANES:DEPTH + (half + 1) * LANES] = low
+
+    def multiply(g, four, parts):
         made = lax.dot_general(
-            had[...], parts[pl.ds(it * 4 * width, 4 * width), :],
+            had[...], parts[four * 4 * width:(four + 1) * 4 * width, :],
             (((1,), (1,)), ((), ())), preferred_element_type=jnp.float32,
         )
-        at = (g * (INNER // 2) + it * 2) * DEPTH
+        at = (g * (INNER // 2) + four * 2) * DEPTH
         table[pl.ds(at, DEPTH), :] = made[:, :LANES]
         table[pl.ds(at + DEPTH, DEPTH), :] = made[:, LANES:]
 
-    both = (parts_a, parts_b)
-    for g in range(CHUNKS + 1):
-        if g < CHUNKS:
-            chunks[g].wait()
-
-        @pl.loop(0, 4)
-        def _(it):
-            if g > 0:
-                multiply(g - 1, it, both[(g - 1) % 2])
-            if g < CHUNKS:
-                prepare(g, it, both[g % 2])
+    def stage(g, before, after):
+        for four in range(4):
+            if before is not None:
+                multiply(g - 1, four, before)
+            if after is not None:
+                prepare(g, four * 16, 0, after)
+                prepare(g, four * 16, 1, after)
+
+    def wait(g):
+        chunk(g).wait()
+
+        @pl.when(g + AHEAD < CHUNKS)
+        def _():
+            chunk(g + AHEAD).start()
+
+    wait(0)
+    stage(0, None, parts_a)
+
+    @pl.loop(0, CHUNKS // 2 - 1)
+    def _(pair):
+        wait(2 * pair + 1)
+        stage(2 * pair + 1, parts_a, parts_b)
+        wait(2 * pair + 2)
+        stage(2 * pair + 2, parts_b, parts_a)
+
+    wait(CHUNKS - 1)
+
+    @pl.when(me < BLOCKS)
+    def _():
+        stage(CHUNKS - 1, parts_a, parts_b)
+
+    @pl.when(me < BLOCKS)
+    def _():
+        stage(CHUNKS, parts_b, None)
+
 
     stretch = table.shape[0] // CHUNKS
     step = 32
@@ -224,7 +248,7 @@
         out_shape=(
             jax.ShapeDtypeStruct((BLOCKS // 2, width, CAPACITY), f32),
             jax.ShapeDtypeStruct((rows_here // 2, LANES), f32),
-            jax.ShapeDtypeStruct((BLOCKS, LANES), i32),
+            jax.ShapeDtypeStruct((2 * BLOCKS, LANES), i32),
             jax.ShapeDtypeStruct((2 * BLOCKS, LANES), f32),
         ),
         in_specs=[ANY] * 4,
@@ -238,7 +262,7 @@
             pltpu.VMEM((DEPTH, 2 * DEPTH), jnp.bfloat16),
             pltpu.VMEM((INNER * width, 2 * DEPTH), jnp.bfloat16),
             pltpu.VMEM((INNER * width, 2 * DEPTH), jnp.bfloat16),
-            pltpu.SMEM((BLOCKS, LANES), i32),
+            pltpu.SMEM((2 * BLOCKS, LANES), i32),
             pltpu.VMEM((BLOCKS // 2 * CAPACITY, LANES), f32),
             pltpu.SemaphoreType.DMA((CHUNKS,)),
             pltpu.SemaphoreType.DMA((3,)),
@@ -258,7 +282,7 @@
         in_specs=[VMEM] * 3,
         out_specs=VMEM,
         scratch_shapes=[
-            pltpu.SMEM((BLOCKS, LANES), jnp.int32),
+            pltpu.SMEM((2 * BLOCKS, LANES), jnp.int32),
             pltpu.VMEM((blocks * CAPACITY, LANES), jnp.float32),
             pltpu.SemaphoreType.DMA,
         ],

time: 42.8 us -> 34 us (0.79)
  Pallas kernels: 23 us -> 14.5 us
    pallas_call x1, Pallas kernels: 18.3 us -> 11.1 us  [transform(): pl.pallas_call(transform_kernel, out_shape=(jax.ShapeDtypeStruct((BLOCKS...]
    pallas_call x1, Pallas kernels: 4.66 us -> 3.43 us  [take(): pl.pallas_call(functools.partial(take_kernel, first), out_shape=jax.Shape...]
  transfers between devices with their start and end apart: 7 -> 7, of which waited for: 5 -> 5; matrix products, arithmetic and copies ran while one was open for 0% -> 0% of each run, Pallas kernels for 11% -> 10%
where the time goes in v3:
time: 34 us; the launch traced here: 33.9 us
  Pallas kernels  14.5 us (43%)
  starting transfers between devices  10.7 us (31%)
  waiting for transfers between devices  7.92 us (23%)
  other arithmetic  0.71 us (2%)
    pallas_call x1, Pallas kernels, transform(): pl.pallas_call(transform_kernel, out_shape=(jax.ShapeDtypeStruct((BLOCKS...  11.1 us
    ppermute x3, starting transfers between devices, shards(): out = out + lax.ppermute(own[step], 'row', shift(step, False))  5.38 us
    ppermute x3, starting transfers between devices, shards(): lax.ppermute(held[step * 4:step * 4 + 4], 'row', shift(step, True))  5.21 us
    ppermute x3, waiting for transfers between devices, shards(): lax.ppermute(held[step * 4:step * 4 + 4], 'row', shift(step, True))  4.57 us
    pallas_call x1, Pallas kernels, take(): pl.pallas_call(functools.partial(take_kernel, first), out_shape=jax.Shape...  3.43 us
    ppermute x3, waiting for transfers between devices, shards(): out = out + lax.ppermute(own[step], 'row', shift(step, False))  3.35 us
  transfers between devices with their start and end apart: 7, of which 5 were waited for; matrix products, arithmetic and copies ran while one was open for 0% of the time, Pallas kernels for 10%

profile of v3, /device:TPU:0, one launch (start us, length us, event | category | flops | bytes accessed | tf_op | source)
XLA Modules:
  0.0 33.9 jit_solution(7254034342140001538)
XLA Ops:
  0.0 11.1 %shard_map.46 = (f32[16,64,128]{2,1,0:T(8,128)S(1)}, f32[16384,128]{1,0:T(8,128)S(1)}, s32[64,128]{1,0:T(8,128)S(1)}, f32[64,128]{1,0:T(8,128)S(1)}) custom-call(f32[64,32768]{1,0:T(8,128)} %x_ref.1, s32[256,128]{1,0:T(8,128)} %bitcast.17, s32[16,128]{1,0:T(8,128)} %bitcast.18, s32[16,128]{1,0:T(8,128)} %bitcast.19), custom_call_target="tpu_custom_call" | custom-call | tf_op jit(solution)/shard_map/pallas_call | solution.py:246
  11.1 0.1 collective-permute-start
  11.2 3.4 %shard_map.47 = f32[16,64,128]{2,1,0:T(8,128)S(1)} custom-call(f32[16384,128]{1,0:T(8,128)S(1)} %get-tuple-element.9.table, s32[64,128]{1,0:T(8,128)S(1)} %get-tuple-element.10.listed_ref, f32[64,128]{1,0:T(8,128)S(1)} %get-tuple-element.11.weight), custom_call_target="tpu_custom_call" | custom-call | bytes 4194304 | tf_op jit(solution)/shard_map/pallas_call | solution.py:279
  14.6 0.0 collective-permute-done
  14.6 0.1 add.21
  14.7 1.6 %collective-permute-start.1 = (f32[4,64,128]{2,1,0:T(8,128)S(1)}, f32[4,64,128]{2,1,0:T(8,128)S(1)}, u32[]{:S(2)}, u32[]{:S(2)}) collective-permute-start(f32[4,64,128]{2,1,0:T(8,128)S(1)} %get-tuple-element.13), channel_id=1, source_target_pairs={{0,32},{4,12},{8,40},{12,20},{16,48},{20,28},{24,56},{28,4},{32,64... | collective-permute-start | bytes 393224 | tf_op jit(solution)/shard_map/ppermute | solution.py:329
  16.4 1.7 %collective-permute-start.3 = (f32[4,64,128]{2,1,0:T(8,128)S(1)}, f32[4,64,128]{2,1,0:T(8,128)S(1)}, u32[]{:S(2)}, u32[]{:S(2)}) collective-permute-start(f32[4,64,128]{2,1,0:T(8,128)S(1)} %get-tuple-element.14), channel_id=1, source_target_pairs={{0,96},{4,28},{8,104},{12,4},{16,112},{20,12},{24,120},{28,20},{32... | collective-permute-start | bytes 393224 | tf_op jit(solution)/shard_map/ppermute | solution.py:329
  18.0 1.9 %collective-permute-start.2 = (f32[4,64,128]{2,1,0:T(8,128)S(1)}, f32[4,64,128]{2,1,0:T(8,128)S(1)}, u32[]{:S(2)}, u32[]{:S(2)}) collective-permute-start(f32[4,64,128]{2,1,0:T(8,128)S(1)} %get-tuple-element.15), channel_id=1, source_target_pairs={{0,64},{4,20},{8,72},{12,28},{16,80},{20,4},{24,88},{28,12},{32,96... | collective-permute-start | bytes 393224 | tf_op jit(solution)/shard_map/ppermute | solution.py:329
  20.0 1.0 %collective-permute-done.1 = f32[4,64,128]{2,1,0:T(8,128)S(1)} collective-permute-done((f32[4,64,128]{2,1,0:T(8,128)S(1)}, f32[4,64,128]{2,1,0:T(8,128)S(1)}, u32[]{:S(2)}, u32[]{:S(2)}) %collective-permute-start.1) | collective-permute-done | bytes 131104 | tf_op jit(solution)/shard_map/ppermute | solution.py:329
  21.0 0.4 %collective-permute-done.3 = f32[4,64,128]{2,1,0:T(8,128)S(1)} collective-permute-done((f32[4,64,128]{2,1,0:T(8,128)S(1)}, f32[4,64,128]{2,1,0:T(8,128)S(1)}, u32[]{:S(2)}, u32[]{:S(2)}) %collective-permute-start.3) | collective-permute-done | bytes 131104 | tf_op jit(solution)/shard_map/ppermute | solution.py:329
  21.4 3.2 %collective-permute-done.2 = f32[4,64,128]{2,1,0:T(8,128)S(1)} collective-permute-done((f32[4,64,128]{2,1,0:T(8,128)S(1)}, f32[4,64,128]{2,1,0:T(8,128)S(1)}, u32[]{:S(2)}, u32[]{:S(2)}) %collective-permute-start.2) | collective-permute-done | bytes 131104 | tf_op jit(solution)/shard_map/ppermute | solution.py:329
  24.6 1.7 %collective-permute-start.4 = (f32[64,128]{1,0:T(8,128)S(1)}, f32[64,128]{1,0:T(8,128)S(1)}, u32[]{:S(2)}, u32[]{:S(2)}) collective-permute-start(f32[64,128]{1,0:T(8,128)S(1)} %get-tuple-element.16), channel_id=1, source_target_pairs={{0,8},{4,36},{8,16},{12,44},{16,24},{20,52},{24,0},{28,60},{32,40}... | collective-permute-start | bytes 98312 | tf_op jit(solution)/shard_map/ppermute | solution.py:332
  26.3 1.6 %collective-permute-start.6 = (f32[64,128]{1,0:T(8,128)S(1)}, f32[64,128]{1,0:T(8,128)S(1)}, u32[]{:S(2)}, u32[]{:S(2)}) collective-permute-start(f32[64,128]{1,0:T(8,128)S(1)} %get-tuple-element.17), channel_id=1, source_target_pairs={{0,24},{4,100},{8,0},{12,108},{16,8},{20,116},{24,16},{28,124},{32... | collective-permute-start | bytes 98312 | tf_op jit(solution)/shard_map/ppermute | solution.py:332
  27.9 2.1 %collective-permute-start.5 = (f32[64,128]{1,0:T(8,128)S(1)}, f32[64,128]{1,0:T(8,128)S(1)}, u32[]{:S(2)}, u32[]{:S(2)}) collective-permute-start(f32[64,128]{1,0:T(8,128)S(1)} %get-tuple-element.18), channel_id=1, source_target_pairs={{0,16},{4,68},{8,24},{12,76},{16,0},{20,84},{24,8},{28,92},{32,48}... | collective-permute-start | bytes 98312 | tf_op jit(solution)/shard_map/ppermute | solution.py:332
  29.9 0.0 collective-permute-done.4
  29.9 0.3 collective-permute-done.6
  30.2 3.1 %collective-permute-done.5 = f32[64,128]{1,0:T(8,128)S(1)} collective-permute-done((f32[64,128]{1,0:T(8,128)S(1)}, f32[64,128]{1,0:T(8,128)S(1)}, u32[]{:S(2)}, u32[]{:S(2)}) %collective-permute-start.5) | collective-permute-done | bytes 32800 | tf_op jit(solution)/shard_map/ppermute | solution.py:332
  33.3 0.6 %fusion.4 = f32[64,128]{1,0:T(8,128)} fusion(f32[64,128]{1,0:T(8,128)S(1)} %collective-permute-done.6, f32[64,128]{1,0:T(8,128)S(1)} %collective-permute-done.5, f32[64,128]{1,0:T(8,128)S(1)} %collective-permute-done.4, f32[4,64,128]{2,1,0:T(8,128)S(1)} %fusion.1), kind=kLoop, calls=%fused_computation.9 | loop fusion | flops 24576 | bytes 163840 | tf_op jit(solution)/shard_map/add | solution.py:332
  (3 shorter events, 0.1 us)
Async XLA Ops:
  11.1 3.5 %collective-permute-start = (f32[16,64,128]{2,1,0:T(8,128)S(1)}, f32[16,64,128]{2,1,0:T(8,128)S(1)}, u32[]{:S(2)}, u32[]{:S(2)}) collective-permute-start(f32[16,64,128]{2,1,0:T(8,128)S(1)} %get-tuple-element.12), channel_id=1, source_target_pairs={{0,4},{4,0},{8,12},{12,8},{16,20},{20,16},{24,28},{28,24},{32,36},... | collective-permute-start | bytes 1572872 | tf_op jit(solution)/shard_map/ppermute | solution.py:325
  14.7 6.2 %collective-permute-start.1 = (f32[4,64,128]{2,1,0:T(8,128)S(1)}, f32[4,64,128]{2,1,0:T(8,128)S(1)}, u32[]{:S(2)}, u32[]{:S(2)}) collective-permute-start(f32[4,64,128]{2,1,0:T(8,128)S(1)} %get-tuple-element.13), channel_id=1, source_target_pairs={{0,32},{4,12},{8,40},{12,20},{16,48},{20,28},{24,56},{28,4},{32,64... | collective-permute-start | bytes 393224 | tf_op jit(solution)/shard_map/ppermute | solution.py:329
  16.4 5.0 %collective-permute-start.3 = (f32[4,64,128]{2,1,0:T(8,128)S(1)}, f32[4,64,128]{2,1,0:T(8,128)S(1)}, u32[]{:S(2)}, u32[]{:S(2)}) collective-permute-start(f32[4,64,128]{2,1,0:T(8,128)S(1)} %get-tuple-element.14), channel_id=1, source_target_pairs={{0,96},{4,28},{8,104},{12,4},{16,112},{20,12},{24,120},{28,20},{32... | collective-permute-start | bytes 393224 | tf_op jit(solution)/shard_map/ppermute | solution.py:329
  18.0 6.5 %collective-permute-start.2 = (f32[4,64,128]{2,1,0:T(8,128)S(1)}, f32[4,64,128]{2,1,0:T(8,128)S(1)}, u32[]{:S(2)}, u32[]{:S(2)}) collective-permute-start(f32[4,64,128]{2,1,0:T(8,128)S(1)} %get-tuple-element.15), channel_id=1, source_target_pairs={{0,64},{4,20},{8,72},{12,28},{16,80},{20,4},{24,88},{28,12},{32,96... | collective-permute-start | bytes 393224 | tf_op jit(solution)/shard_map/ppermute | solution.py:329
  24.6 5.4 %collective-permute-start.4 = (f32[64,128]{1,0:T(8,128)S(1)}, f32[64,128]{1,0:T(8,128)S(1)}, u32[]{:S(2)}, u32[]{:S(2)}) collective-permute-start(f32[64,128]{1,0:T(8,128)S(1)} %get-tuple-element.16), channel_id=1, source_target_pairs={{0,8},{4,36},{8,16},{12,44},{16,24},{20,52},{24,0},{28,60},{32,40}... | collective-permute-start | bytes 98312 | tf_op jit(solution)/shard_map/ppermute | solution.py:332
  26.3 3.9 %collective-permute-start.6 = (f32[64,128]{1,0:T(8,128)S(1)}, f32[64,128]{1,0:T(8,128)S(1)}, u32[]{:S(2)}, u32[]{:S(2)}) collective-permute-start(f32[64,128]{1,0:T(8,128)S(1)} %get-tuple-element.17), channel_id=1, source_target_pairs={{0,24},{4,100},{8,0},{12,108},{16,8},{20,116},{24,16},{28,124},{32... | collective-permute-start | bytes 98312 | tf_op jit(solution)/shard_map/ppermute | solution.py:332
  27.9 5.4 %collective-permute-start.5 = (f32[64,128]{1,0:T(8,128)S(1)}, f32[64,128]{1,0:T(8,128)S(1)}, u32[]{:S(2)}, u32[]{:S(2)}) collective-permute-start(f32[64,128]{1,0:T(8,128)S(1)} %get-tuple-element.18), channel_id=1, source_target_pairs={{0,16},{4,68},{8,24},{12,76},{16,0},{20,84},{24,8},{28,92},{32,48}... | collective-permute-start | bytes 98312 | tf_op jit(solution)/shard_map/ppermute | solution.py:332

commit v4 on v3

--- a/solution.py
+++ b/solution.py
@@ -228,10 +228,17 @@
 
 
 def take_kernel(first, table, listed_ref, weight, out_ref, listed, rows, l_sem):
-    listing = pltpu.make_async_copy(listed_ref, listed, l_sem)
-    listing.start()
-    listing.wait()
     blocks = out_ref.shape[0]
+    copies = [
+        pltpu.make_async_copy(
+            listed_ref.at[at:at + BLOCKS // 2], listed.at[at:at + BLOCKS // 2], l_sem.at[n]
+        )
+        for n, at in enumerate((0, BLOCKS))
+    ]
+    for copy in copies:
+        copy.start()
+    for copy in copies:
+        copy.wait()
     take_rows(first, blocks, table, listed, rows)
     turn_rows(first, blocks, rows, weight, out_ref)
 
@@ -284,7 +291,7 @@
         scratch_shapes=[
             pltpu.SMEM((2 * BLOCKS, LANES), jnp.int32),
             pltpu.VMEM((blocks * CAPACITY, LANES), jnp.float32),
-            pltpu.SemaphoreType.DMA,
+            pltpu.SemaphoreType.DMA((2,)),
         ],
         compiler_params=pltpu.CompilerParams(vmem_limit_bytes=24 << 20),
         cost_estimate=pl.CostEstimate(
@@ -322,14 +329,19 @@
         picks.reshape(-1, LANES),
         owners.reshape(-1, LANES),
     )
-    held = lax.ppermute(send, "row", core_swap())
-    held = take(0, BLOCKS // 2, width, *made) + held
-    own = held[0:4]
-    for step in (1, 2, 3):
-        own = own + lax.ppermute(held[step * 4:step * 4 + 4], "row", shift(step, True))
+    crossed = lax.ppermute(send, "row", core_swap())
+    far = take(4, BLOCKS // 2 - 4, width, *made) + crossed[4:]
+    moved = [
+        lax.ppermute(far[step * 4 - 4:step * 4], "row", shift(step, True))
+        for step in (1, 3, 2)
+    ]
+    own = take(0, 4, width, *made) + crossed[:4]
+    for part in moved:
+        own = own + part
+    moved = [lax.ppermute(own[step], "row", shift(step, False)) for step in (1, 3, 2)]
     out = own[0]
-    for step in (1, 2, 3):
-        out = out + lax.ppermute(own[step], "row", shift(step, False))
+    for part in moved:
+        out = out + part
     return out
 
 

time: 34 us -> 32.5 us (0.956)
  waiting for transfers between devices: 7.92 us -> 4.77 us
  starting transfers between devices: 10.7 us -> 11.7 us
  Pallas kernels: 14.5 us -> 15.1 us
    ppermute x7, waiting for transfers between devices: 7.92 us -> 4.77 us  [the longest x3 2.56 us: shards(): lax.ppermute(own[step], 'row', shift(step, False))]
    ppermute x7, starting transfers between devices: 10.7 us -> 11.7 us  [the longest x3 5.9 us: shards(): lax.ppermute(own[step], 'row', shift(step, False))]
    pallas_call x1 -> x2, Pallas kernels: 3.43 us -> 3.9 us  [take(): pl.pallas_call(functools.partial(take_kernel, first), out_shape=jax.Shape...]
  transfers between devices with their start and end apart: 7 -> 7, of which waited for: 5 -> 4; matrix products, arithmetic and copies ran while one was open for 0% -> 0% of each run, Pallas kernels for 10% -> 12%
where the time goes in v4:
time: 32.5 us; the launch traced here: 32.4 us
  Pallas kernels  15.1 us (46%)
  starting transfers between devices  11.7 us (36%)
  waiting for transfers between devices  4.77 us (15%)
  other arithmetic  0.71 us (2%)
    pallas_call x1, Pallas kernels, transform(): pl.pallas_call(transform_kernel, out_shape=(jax.ShapeDtypeStruct((BLOCKS...  11.2 us
    ppermute x3, starting transfers between devices, shards(): lax.ppermute(own[step], 'row', shift(step, False))  5.9 us
    ppermute x3, starting transfers between devices, shards(): lax.ppermute(far[step * 4 - 4:step * 4], 'row', shift(step, True))  5.76 us
    pallas_call x2, Pallas kernels, take(): pl.pallas_call(functools.partial(take_kernel, first), out_shape=jax.Shape...  3.9 us
    ppermute x3, waiting for transfers between devices, shards(): lax.ppermute(own[step], 'row', shift(step, False))  2.56 us
    ppermute x3, waiting for transfers between devices, shards(): lax.ppermute(far[step * 4 - 4:step * 4], 'row', shift(step, True))  2.21 us
  transfers between devices with their start and end apart: 7, of which 4 were waited for; matrix products, arithmetic and copies ran while one was open for 0% of the time, Pallas kernels for 12%

profile of v4, /device:TPU:0, one launch (start us, length us, event | category | flops | bytes accessed | tf_op | source)
XLA Modules:
  0.0 32.4 jit_solution(16560044146032643618)
XLA Ops:
  0.0 11.2 %shard_map.46 = (f32[16,64,128]{2,1,0:T(8,128)S(1)}, f32[16384,128]{1,0:T(8,128)S(1)}, s32[64,128]{1,0:T(8,128)S(1)}, f32[64,128]{1,0:T(8,128)S(1)}) custom-call(f32[64,32768]{1,0:T(8,128)} %x_ref.1, s32[256,128]{1,0:T(8,128)} %bitcast.17, s32[16,128]{1,0:T(8,128)} %bitcast.18, s32[16,128]{1,0:T(8,128)} %bitcast.19), custom_call_target="tpu_custom_call" | custom-call | tf_op jit(solution)/shard_map/pallas_call | solution.py:253
  11.2 0.1 collective-permute-start
  11.3 2.5 %shard_map.48 = f32[12,64,128]{2,1,0:T(8,128)S(1)} custom-call(f32[16384,128]{1,0:T(8,128)S(1)} %get-tuple-element.9.table, s32[64,128]{1,0:T(8,128)S(1)} %get-tuple-element.10.listed_ref, f32[64,128]{1,0:T(8,128)S(1)} %get-tuple-element.11.weight), custom_call_target="tpu_custom_call" | custom-call | bytes 3145728 | tf_op jit(solution)/shard_map/pallas_call | solution.py:286
  13.8 0.0 collective-permute-done
  13.9 1.7 %collective-permute-start.1 = (f32[4,64,128]{2,1,0:T(8,128)S(1)}, f32[4,64,128]{2,1,0:T(8,128)S(1)}, u32[]{:S(2)}, u32[]{:S(2)}) collective-permute-start(f32[4,64,128]{2,1,0:T(8,128)S(1)} %get-tuple-element.13), channel_id=1, source_target_pairs={{0,32},{4,12},{8,40},{12,20},{16,48},{20,28},{24,56},{28,4},{32,64... | collective-permute-start | bytes 393224 | tf_op jit(solution)/shard_map/ppermute | solution.py:335
  15.6 2.7 %collective-permute-start.3 = (f32[4,64,128]{2,1,0:T(8,128)S(1)}, f32[4,64,128]{2,1,0:T(8,128)S(1)}, u32[]{:S(2)}, u32[]{:S(2)}) collective-permute-start(f32[4,64,128]{2,1,0:T(8,128)S(1)} %get-tuple-element.14), channel_id=1, source_target_pairs={{0,64},{4,20},{8,72},{12,28},{16,80},{20,4},{24,88},{28,12},{32,96... | collective-permute-start | bytes 393224 | tf_op jit(solution)/shard_map/ppermute | solution.py:335
  18.3 1.4 %collective-permute-start.2 = (f32[4,64,128]{2,1,0:T(8,128)S(1)}, f32[4,64,128]{2,1,0:T(8,128)S(1)}, u32[]{:S(2)}, u32[]{:S(2)}) collective-permute-start(f32[4,64,128]{2,1,0:T(8,128)S(1)} %get-tuple-element.15), channel_id=1, source_target_pairs={{0,96},{4,28},{8,104},{12,4},{16,112},{20,12},{24,120},{28,20},{32... | collective-permute-start | bytes 393224 | tf_op jit(solution)/shard_map/ppermute | solution.py:335
  19.7 1.4 %shard_map.47 = f32[4,64,128]{2,1,0:T(8,128)S(1)} custom-call(f32[16384,128]{1,0:T(8,128)S(1)} %get-tuple-element.9.table, s32[64,128]{1,0:T(8,128)S(1)} %get-tuple-element.10.listed_ref, f32[64,128]{1,0:T(8,128)S(1)} %get-tuple-element.11.weight), custom_call_target="tpu_custom_call" | custom-call | bytes 1048576 | tf_op jit(solution)/shard_map/pallas_call | solution.py:286
  21.1 0.0 collective-permute-done.1
  21.1 1.6 %collective-permute-done.3 = f32[4,64,128]{2,1,0:T(8,128)S(1)} collective-permute-done((f32[4,64,128]{2,1,0:T(8,128)S(1)}, f32[4,64,128]{2,1,0:T(8,128)S(1)}, u32[]{:S(2)}, u32[]{:S(2)}) %collective-permute-start.3) | collective-permute-done | bytes 131104 | tf_op jit(solution)/shard_map/ppermute | solution.py:335
  22.6 0.6 %collective-permute-done.2 = f32[4,64,128]{2,1,0:T(8,128)S(1)} collective-permute-done((f32[4,64,128]{2,1,0:T(8,128)S(1)}, f32[4,64,128]{2,1,0:T(8,128)S(1)}, u32[]{:S(2)}, u32[]{:S(2)}) %collective-permute-start.2) | collective-permute-done | bytes 131104 | tf_op jit(solution)/shard_map/ppermute | solution.py:335
  23.3 1.6 %collective-permute-start.4 = (f32[64,128]{1,0:T(8,128)S(1)}, f32[64,128]{1,0:T(8,128)S(1)}, u32[]{:S(2)}, u32[]{:S(2)}) collective-permute-start(f32[64,128]{1,0:T(8,128)S(1)} %get-tuple-element.16), channel_id=1, source_target_pairs={{0,8},{4,36},{8,16},{12,44},{16,24},{20,52},{24,0},{28,60},{32,40}... | collective-permute-start | bytes 98312 | tf_op jit(solution)/shard_map/ppermute | solution.py:341
  25.0 2.9 %collective-permute-start.6 = (f32[64,128]{1,0:T(8,128)S(1)}, f32[64,128]{1,0:T(8,128)S(1)}, u32[]{:S(2)}, u32[]{:S(2)}) collective-permute-start(f32[64,128]{1,0:T(8,128)S(1)} %get-tuple-element.17), channel_id=1, source_target_pairs={{0,16},{4,68},{8,24},{12,76},{16,0},{20,84},{24,8},{28,92},{32,48}... | collective-permute-start | bytes 98312 | tf_op jit(solution)/shard_map/ppermute | solution.py:341
  27.9 1.3 %collective-permute-start.5 = (f32[64,128]{1,0:T(8,128)S(1)}, f32[64,128]{1,0:T(8,128)S(1)}, u32[]{:S(2)}, u32[]{:S(2)}) collective-permute-start(f32[64,128]{1,0:T(8,128)S(1)} %get-tuple-element.18), channel_id=1, source_target_pairs={{0,24},{4,100},{8,0},{12,108},{16,8},{20,116},{24,16},{28,124},{32... | collective-permute-start | bytes 98312 | tf_op jit(solution)/shard_map/ppermute | solution.py:341
  29.2 0.0 collective-permute-done.4
  29.2 1.2 %collective-permute-done.6 = f32[64,128]{1,0:T(8,128)S(1)} collective-permute-done((f32[64,128]{1,0:T(8,128)S(1)}, f32[64,128]{1,0:T(8,128)S(1)}, u32[]{:S(2)}, u32[]{:S(2)}) %collective-permute-start.6) | collective-permute-done | bytes 32800 | tf_op jit(solution)/shard_map/ppermute | solution.py:341
  30.4 1.4 %collective-permute-done.5 = f32[64,128]{1,0:T(8,128)S(1)} collective-permute-done((f32[64,128]{1,0:T(8,128)S(1)}, f32[64,128]{1,0:T(8,128)S(1)}, u32[]{:S(2)}, u32[]{:S(2)}) %collective-permute-start.5) | collective-permute-done | bytes 32800 | tf_op jit(solution)/shard_map/ppermute | solution.py:341
  31.8 0.6 %fusion.5 = f32[64,128]{1,0:T(8,128)} fusion(f32[64,128]{1,0:T(8,128)S(1)} %collective-permute-done.6, f32[64,128]{1,0:T(8,128)S(1)} %collective-permute-done.5, f32[64,128]{1,0:T(8,128)S(1)} %collective-permute-done.4, f32[4,64,128]{2,1,0:T(8,128)S(1)} %fusion.2), kind=kLoop, calls=%fused_computation.11 | loop fusion | flops 24576 | bytes 163840 | tf_op jit(solution)/shard_map/add | solution.py:344
  (4 shorter events, 0.1 us)
Async XLA Ops:
  11.2 2.6 %collective-permute-start = (f32[16,64,128]{2,1,0:T(8,128)S(1)}, f32[16,64,128]{2,1,0:T(8,128)S(1)}, u32[]{:S(2)}, u32[]{:S(2)}) collective-permute-start(f32[16,64,128]{2,1,0:T(8,128)S(1)} %get-tuple-element.12), channel_id=1, source_target_pairs={{0,4},{4,0},{8,12},{12,8},{16,20},{20,16},{24,28},{28,24},{32,36},... | collective-permute-start | bytes 1572872 | tf_op jit(solution)/shard_map/ppermute | solution.py:332
  13.9 7.2 %collective-permute-start.1 = (f32[4,64,128]{2,1,0:T(8,128)S(1)}, f32[4,64,128]{2,1,0:T(8,128)S(1)}, u32[]{:S(2)}, u32[]{:S(2)}) collective-permute-start(f32[4,64,128]{2,1,0:T(8,128)S(1)} %get-tuple-element.13), channel_id=1, source_target_pairs={{0,32},{4,12},{8,40},{12,20},{16,48},{20,28},{24,56},{28,4},{32,64... | collective-permute-start | bytes 393224 | tf_op jit(solution)/shard_map/ppermute | solution.py:335
  15.6 7.1 %collective-permute-start.3 = (f32[4,64,128]{2,1,0:T(8,128)S(1)}, f32[4,64,128]{2,1,0:T(8,128)S(1)}, u32[]{:S(2)}, u32[]{:S(2)}) collective-permute-start(f32[4,64,128]{2,1,0:T(8,128)S(1)} %get-tuple-element.14), channel_id=1, source_target_pairs={{0,64},{4,20},{8,72},{12,28},{16,80},{20,4},{24,88},{28,12},{32,96... | collective-permute-start | bytes 393224 | tf_op jit(solution)/shard_map/ppermute | solution.py:335
  18.3 5.0 %collective-permute-start.2 = (f32[4,64,128]{2,1,0:T(8,128)S(1)}, f32[4,64,128]{2,1,0:T(8,128)S(1)}, u32[]{:S(2)}, u32[]{:S(2)}) collective-permute-start(f32[4,64,128]{2,1,0:T(8,128)S(1)} %get-tuple-element.15), channel_id=1, source_target_pairs={{0,96},{4,28},{8,104},{12,4},{16,112},{20,12},{24,120},{28,20},{32... | collective-permute-start | bytes 393224 | tf_op jit(solution)/shard_map/ppermute | solution.py:335
  23.3 5.9 %collective-permute-start.4 = (f32[64,128]{1,0:T(8,128)S(1)}, f32[64,128]{1,0:T(8,128)S(1)}, u32[]{:S(2)}, u32[]{:S(2)}) collective-permute-start(f32[64,128]{1,0:T(8,128)S(1)} %get-tuple-element.16), channel_id=1, source_target_pairs={{0,8},{4,36},{8,16},{12,44},{16,24},{20,52},{24,0},{28,60},{32,40}... | collective-permute-start | bytes 98312 | tf_op jit(solution)/shard_map/ppermute | solution.py:341
  25.0 5.4 %collective-permute-start.6 = (f32[64,128]{1,0:T(8,128)S(1)}, f32[64,128]{1,0:T(8,128)S(1)}, u32[]{:S(2)}, u32[]{:S(2)}) collective-permute-start(f32[64,128]{1,0:T(8,128)S(1)} %get-tuple-element.17), channel_id=1, source_target_pairs={{0,16},{4,68},{8,24},{12,76},{16,0},{20,84},{24,8},{28,92},{32,48}... | collective-permute-start | bytes 98312 | tf_op jit(solution)/shard_map/ppermute | solution.py:341
  27.9 3.9 %collective-permute-start.5 = (f32[64,128]{1,0:T(8,128)S(1)}, f32[64,128]{1,0:T(8,128)S(1)}, u32[]{:S(2)}, u32[]{:S(2)}) collective-permute-start(f32[64,128]{1,0:T(8,128)S(1)} %get-tuple-element.18), channel_id=1, source_target_pairs={{0,24},{4,100},{8,0},{12,108},{16,8},{20,116},{24,16},{28,124},{32... | collective-permute-start | bytes 98312 | tf_op jit(solution)/shard_map/ppermute | solution.py:341

commit v5 on v4

--- a/solution.py
+++ b/solution.py
@@ -104,9 +104,9 @@
 def turn_rows(first, blocks, rows, weight, out_ref):
     width = out_ref.shape[1]
 
-    @pl.loop(0, blocks // 2)
-    def _(pair):
-        for b in (2 * pair, 2 * pair + 1):
+    @pl.loop(0, blocks // 4)
+    def _(group):
+        for b in [4 * group + n for n in range(4)]:
             turned = rows[pl.ds(b * CAPACITY, CAPACITY), :].T
             even = weight[pl.ds(first + b, 1), :]
             odd = weight[pl.ds(BLOCKS + first + b, 1), :]
@@ -145,8 +145,8 @@
     i = lax.broadcasted_iota(jnp.int32, (DEPTH, DEPTH), 0)
     k = lax.broadcasted_iota(jnp.int32, (DEPTH, DEPTH), 1)
     matrix = (1 - 2 * parity(i & k, 8)).astype(jnp.float32).astype(jnp.bfloat16)
-    had[:, :DEPTH] = matrix
-    had[:, DEPTH:] = matrix
+    had[:DEPTH, :DEPTH] = matrix
+    had[:DEPTH, DEPTH:] = matrix
     small[0].wait()
     small[1].wait()
     list_samples(me, picks[...], owners[...], rows_here, listed_ref, weight)
@@ -155,42 +155,48 @@
     small[2].wait()
     signs[...] = (1 - 2 * bits[...]).astype(jnp.float32)
 
-    def prepare(g, c, half, parts):
+    def prepare(g, piece, parts):
+        c, half = piece // 2 * 16, piece % 2
         values = []
         for j in range(INNER):
             at = j * DEPTH + half * LANES
             sign = signs[pl.ds(g * (span // LANES) + at // LANES, 1), :]
             values.append(x_buf[g, c:c + 16, at:at + LANES] * sign)
-        for j, value in enumerate(butterflies(values)):
+        for j, value in enumerate(butterflies(values[:8]) + butterflies(values[8:])):
             high = value.astype(jnp.bfloat16)
             low = (value - high.astype(jnp.float32)).astype(jnp.bfloat16)
             at = slice(j * width + c, j * width + c + 16)
             parts[at, half * LANES:(half + 1) * LANES] = high
             parts[at, DEPTH + half * LANES:DEPTH + (half + 1) * LANES] = low
+        had[pl.ds(DEPTH + (g >> 8) * 16, 16), :LANES] = low
+        x_buf[CHUNKS + (g >> 8), :16, :LANES] = low.astype(jnp.float32)
 
     def multiply(g, four, parts):
         made = lax.dot_general(
-            had[...], parts[four * 4 * width:(four + 1) * 4 * width, :],
+            had[:DEPTH], parts[four * 4 * width:(four + 1) * 4 * width, :],
             (((1,), (1,)), ((), ())), preferred_element_type=jnp.float32,
         )
         at = (g * (INNER // 2) + four * 2) * DEPTH
         table[pl.ds(at, DEPTH), :] = made[:, :LANES]
         table[pl.ds(at + DEPTH, DEPTH), :] = made[:, LANES:]
 
+    def wait(g):
+        chunk(g).wait()
+
+        @pl.when(g + AHEAD < CHUNKS)
+        def _():
+            chunk(g + AHEAD).start()
+
+    pieces = width // 8
+    quads = INNER // 4
+
     def stage(g, before, after):
-        for four in range(4):
+        for four in range(quads):
             if before is not None:
                 multiply(g - 1, four, before)
             if after is not None:
-                prepare(g, four * 16, 0, after)
-                prepare(g, four * 16, 1, after)
-
-    def wait(g):
-        chunk(g).wait()
-
-        @pl.when(g + AHEAD < CHUNKS)
-        def _():
-            chunk(g + AHEAD).start()
+                for piece in range(four * pieces // quads, (four + 1) * pieces // quads):
+                    prepare(g, piece, after)
 
     wait(0)
     stage(0, None, parts_a)
@@ -203,22 +209,15 @@
         stage(2 * pair + 2, parts_b, parts_a)
 
     wait(CHUNKS - 1)
-
-    @pl.when(me < BLOCKS)
-    def _():
-        stage(CHUNKS - 1, parts_a, parts_b)
-
-    @pl.when(me < BLOCKS)
-    def _():
-        stage(CHUNKS, parts_b, None)
-
-
-    stretch = table.shape[0] // CHUNKS
-    step = 32
-
-    @pl.loop(0, stretch // step)
+    stage(CHUNKS - 1, parts_a, parts_b)
+    stage(CHUNKS, parts_b, None)
+
+    stretch = table.shape[0] // 16
+    step = 16
+
+    @pl.loop(0, stretch // step, unroll=2)
     def _(at):
-        values = [table[pl.ds(g * stretch + at * step, step), :] for g in range(CHUNKS)]
+        values = [table[pl.ds(g * stretch + at * step, step), :] for g in range(16)]
         for g, value in enumerate(butterflies(values)):
             table[pl.ds(g * stretch + at * step, step), :] = value
 
@@ -261,12 +260,12 @@
         in_specs=[ANY] * 4,
         out_specs=(VMEM,) * 4,
         scratch_shapes=[
-            pltpu.VMEM((CHUNKS, width, rows_here // CHUNKS), f32),
+            pltpu.VMEM((CHUNKS + 1, width, rows_here // CHUNKS), f32),
             pltpu.VMEM(bits.shape, i32),
             pltpu.VMEM(picks.shape, i32),
             pltpu.VMEM(owners.shape, i32),
             pltpu.VMEM(bits.shape, f32),
-            pltpu.VMEM((DEPTH, 2 * DEPTH), jnp.bfloat16),
+            pltpu.VMEM((DEPTH + 16, 2 * DEPTH), jnp.bfloat16),
             pltpu.VMEM((INNER * width, 2 * DEPTH), jnp.bfloat16),
             pltpu.VMEM((INNER * width, 2 * DEPTH), jnp.bfloat16),
             pltpu.SMEM((2 * BLOCKS, LANES), i32),

time: 32.5 us -> 30.8 us (0.948)
  Pallas kernels: 15.1 us -> 13.2 us
    pallas_call x1, Pallas kernels: 11.2 us -> 9.57 us  [transform(): pl.pallas_call(transform_kernel, out_shape=(jax.ShapeDtypeStruct((BLOCKS...]
where the time goes in v5:
time: 30.8 us; the launch traced here: 30.6 us
  Pallas kernels  13.2 us (43%)
  starting transfers between devices  11.8 us (38%)
  waiting for transfers between devices  4.82 us (16%)
  other arithmetic  0.71 us (2%)
    pallas_call x1, Pallas kernels, transform(): pl.pallas_call(transform_kernel, out_shape=(jax.ShapeDtypeStruct((BLOCKS...  9.57 us
    ppermute x3, starting transfers between devices, shards(): lax.ppermute(own[step], 'row', shift(step, False))  5.9 us
    ppermute x3, starting transfers between devices, shards(): lax.ppermute(far[step * 4 - 4:step * 4], 'row', shift(step, True))  5.84 us
    pallas_call x2, Pallas kernels, take(): pl.pallas_call(functools.partial(take_kernel, first), out_shape=jax.Shape...  3.6 us
    ppermute x3, waiting for transfers between devices, shards(): lax.ppermute(own[step], 'row', shift(step, False))  2.56 us
    ppermute x3, waiting for transfers between devices, shards(): lax.ppermute(far[step * 4 - 4:step * 4], 'row', shift(step, True))  2.25 us
    add x1, other arithmetic, shards(): out = out + part  0.62 us
  transfers between devices with their start and end apart: 7, of which 4 were waited for; matrix products, arithmetic and copies ran while one was open for 0% of the time, Pallas kernels for 12%

profile of v5, /device:TPU:0, one launch (start us, length us, event | category | flops | bytes accessed | tf_op | source)
XLA Modules:
  0.0 30.6 jit_solution(3394217782986073038)
XLA Ops:
  0.0 9.6 %shard_map.46 = (f32[16,64,128]{2,1,0:T(8,128)S(1)}, f32[16384,128]{1,0:T(8,128)S(1)}, s32[64,128]{1,0:T(8,128)S(1)}, f32[64,128]{1,0:T(8,128)S(1)}) custom-call(f32[64,32768]{1,0:T(8,128)} %x_ref.1, s32[256,128]{1,0:T(8,128)} %bitcast.17, s32[16,128]{1,0:T(8,128)} %bitcast.18, s32[16,128]{1,0:T(8,128)} %bitcast.19), custom_call_target="tpu_custom_call" | custom-call | tf_op jit(solution)/shard_map/pallas_call | solution.py:252
  9.6 0.1 collective-permute-start
  9.7 2.3 %shard_map.48 = f32[12,64,128]{2,1,0:T(8,128)S(1)} custom-call(f32[16384,128]{1,0:T(8,128)S(1)} %get-tuple-element.9.table, s32[64,128]{1,0:T(8,128)S(1)} %get-tuple-element.10.listed_ref, f32[64,128]{1,0:T(8,128)S(1)} %get-tuple-element.11.weight), custom_call_target="tpu_custom_call" | custom-call | bytes 3145728 | tf_op jit(solution)/shard_map/pallas_call | solution.py:285
  12.0 0.0 collective-permute-done
  12.1 1.5 %collective-permute-start.1 = (f32[4,64,128]{2,1,0:T(8,128)S(1)}, f32[4,64,128]{2,1,0:T(8,128)S(1)}, u32[]{:S(2)}, u32[]{:S(2)}) collective-permute-start(f32[4,64,128]{2,1,0:T(8,128)S(1)} %get-tuple-element.13), channel_id=1, source_target_pairs={{0,32},{4,12},{8,40},{12,20},{16,48},{20,28},{24,56},{28,4},{32,64... | collective-permute-start | bytes 393224 | tf_op jit(solution)/shard_map/ppermute | solution.py:334
  13.6 2.9 %collective-permute-start.3 = (f32[4,64,128]{2,1,0:T(8,128)S(1)}, f32[4,64,128]{2,1,0:T(8,128)S(1)}, u32[]{:S(2)}, u32[]{:S(2)}) collective-permute-start(f32[4,64,128]{2,1,0:T(8,128)S(1)} %get-tuple-element.14), channel_id=1, source_target_pairs={{0,64},{4,20},{8,72},{12,28},{16,80},{20,4},{24,88},{28,12},{32,96... | collective-permute-start | bytes 393224 | tf_op jit(solution)/shard_map/ppermute | solution.py:334
  16.5 1.4 %collective-permute-start.2 = (f32[4,64,128]{2,1,0:T(8,128)S(1)}, f32[4,64,128]{2,1,0:T(8,128)S(1)}, u32[]{:S(2)}, u32[]{:S(2)}) collective-permute-start(f32[4,64,128]{2,1,0:T(8,128)S(1)} %get-tuple-element.15), channel_id=1, source_target_pairs={{0,96},{4,28},{8,104},{12,4},{16,112},{20,12},{24,120},{28,20},{32... | collective-permute-start | bytes 393224 | tf_op jit(solution)/shard_map/ppermute | solution.py:334
  17.9 1.3 %shard_map.47 = f32[4,64,128]{2,1,0:T(8,128)S(1)} custom-call(f32[16384,128]{1,0:T(8,128)S(1)} %get-tuple-element.9.table, s32[64,128]{1,0:T(8,128)S(1)} %get-tuple-element.10.listed_ref, f32[64,128]{1,0:T(8,128)S(1)} %get-tuple-element.11.weight), custom_call_target="tpu_custom_call" | custom-call | bytes 1048576 | tf_op jit(solution)/shard_map/pallas_call | solution.py:285
  19.2 0.0 collective-permute-done.1
  19.2 1.6 %collective-permute-done.3 = f32[4,64,128]{2,1,0:T(8,128)S(1)} collective-permute-done((f32[4,64,128]{2,1,0:T(8,128)S(1)}, f32[4,64,128]{2,1,0:T(8,128)S(1)}, u32[]{:S(2)}, u32[]{:S(2)}) %collective-permute-start.3) | collective-permute-done | bytes 131104 | tf_op jit(solution)/shard_map/ppermute | solution.py:334
  20.9 0.6 %collective-permute-done.2 = f32[4,64,128]{2,1,0:T(8,128)S(1)} collective-permute-done((f32[4,64,128]{2,1,0:T(8,128)S(1)}, f32[4,64,128]{2,1,0:T(8,128)S(1)}, u32[]{:S(2)}, u32[]{:S(2)}) %collective-permute-start.2) | collective-permute-done | bytes 131104 | tf_op jit(solution)/shard_map/ppermute | solution.py:334
  21.5 1.6 %collective-permute-start.4 = (f32[64,128]{1,0:T(8,128)S(1)}, f32[64,128]{1,0:T(8,128)S(1)}, u32[]{:S(2)}, u32[]{:S(2)}) collective-permute-start(f32[64,128]{1,0:T(8,128)S(1)} %get-tuple-element.16), channel_id=1, source_target_pairs={{0,8},{4,36},{8,16},{12,44},{16,24},{20,52},{24,0},{28,60},{32,40}... | collective-permute-start | bytes 98312 | tf_op jit(solution)/shard_map/ppermute | solution.py:340
  23.2 2.9 %collective-permute-start.6 = (f32[64,128]{1,0:T(8,128)S(1)}, f32[64,128]{1,0:T(8,128)S(1)}, u32[]{:S(2)}, u32[]{:S(2)}) collective-permute-start(f32[64,128]{1,0:T(8,128)S(1)} %get-tuple-element.17), channel_id=1, source_target_pairs={{0,16},{4,68},{8,24},{12,76},{16,0},{20,84},{24,8},{28,92},{32,48}... | collective-permute-start | bytes 98312 | tf_op jit(solution)/shard_map/ppermute | solution.py:340
  26.1 1.3 %collective-permute-start.5 = (f32[64,128]{1,0:T(8,128)S(1)}, f32[64,128]{1,0:T(8,128)S(1)}, u32[]{:S(2)}, u32[]{:S(2)}) collective-permute-start(f32[64,128]{1,0:T(8,128)S(1)} %get-tuple-element.18), channel_id=1, source_target_pairs={{0,24},{4,100},{8,0},{12,108},{16,8},{20,116},{24,16},{28,124},{32... | collective-permute-start | bytes 98312 | tf_op jit(solution)/shard_map/ppermute | solution.py:340
  27.4 0.0 collective-permute-done.4
  27.4 1.2 %collective-permute-done.6 = f32[64,128]{1,0:T(8,128)S(1)} collective-permute-done((f32[64,128]{1,0:T(8,128)S(1)}, f32[64,128]{1,0:T(8,128)S(1)}, u32[]{:S(2)}, u32[]{:S(2)}) %collective-permute-start.6) | collective-permute-done | bytes 32800 | tf_op jit(solution)/shard_map/ppermute | solution.py:340
  28.6 1.4 %collective-permute-done.5 = f32[64,128]{1,0:T(8,128)S(1)} collective-permute-done((f32[64,128]{1,0:T(8,128)S(1)}, f32[64,128]{1,0:T(8,128)S(1)}, u32[]{:S(2)}, u32[]{:S(2)}) %collective-permute-start.5) | collective-permute-done | bytes 32800 | tf_op jit(solution)/shard_map/ppermute | solution.py:340
  30.0 0.6 %fusion.5 = f32[64,128]{1,0:T(8,128)} fusion(f32[64,128]{1,0:T(8,128)S(1)} %collective-permute-done.6, f32[64,128]{1,0:T(8,128)S(1)} %collective-permute-done.5, f32[64,128]{1,0:T(8,128)S(1)} %collective-permute-done.4, f32[4,64,128]{2,1,0:T(8,128)S(1)} %fusion.2), kind=kLoop, calls=%fused_computation.11 | loop fusion | flops 24576 | bytes 163840 | tf_op jit(solution)/shard_map/add | solution.py:343
  (4 shorter events, 0.1 us)
Async XLA Ops:
  9.6 2.4 %collective-permute-start = (f32[16,64,128]{2,1,0:T(8,128)S(1)}, f32[16,64,128]{2,1,0:T(8,128)S(1)}, u32[]{:S(2)}, u32[]{:S(2)}) collective-permute-start(f32[16,64,128]{2,1,0:T(8,128)S(1)} %get-tuple-element.12), channel_id=1, source_target_pairs={{0,4},{4,0},{8,12},{12,8},{16,20},{20,16},{24,28},{28,24},{32,36},... | collective-permute-start | bytes 1572872 | tf_op jit(solution)/shard_map/ppermute | solution.py:331
  12.1 7.1 %collective-permute-start.1 = (f32[4,64,128]{2,1,0:T(8,128)S(1)}, f32[4,64,128]{2,1,0:T(8,128)S(1)}, u32[]{:S(2)}, u32[]{:S(2)}) collective-permute-start(f32[4,64,128]{2,1,0:T(8,128)S(1)} %get-tuple-element.13), channel_id=1, source_target_pairs={{0,32},{4,12},{8,40},{12,20},{16,48},{20,28},{24,56},{28,4},{32,64... | collective-permute-start | bytes 393224 | tf_op jit(solution)/shard_map/ppermute | solution.py:334
  13.6 7.3 %collective-permute-start.3 = (f32[4,64,128]{2,1,0:T(8,128)S(1)}, f32[4,64,128]{2,1,0:T(8,128)S(1)}, u32[]{:S(2)}, u32[]{:S(2)}) collective-permute-start(f32[4,64,128]{2,1,0:T(8,128)S(1)} %get-tuple-element.14), channel_id=1, source_target_pairs={{0,64},{4,20},{8,72},{12,28},{16,80},{20,4},{24,88},{28,12},{32,96... | collective-permute-start | bytes 393224 | tf_op jit(solution)/shard_map/ppermute | solution.py:334
  16.5 5.0 %collective-permute-start.2 = (f32[4,64,128]{2,1,0:T(8,128)S(1)}, f32[4,64,128]{2,1,0:T(8,128)S(1)}, u32[]{:S(2)}, u32[]{:S(2)}) collective-permute-start(f32[4,64,128]{2,1,0:T(8,128)S(1)} %get-tuple-element.15), channel_id=1, source_target_pairs={{0,96},{4,28},{8,104},{12,4},{16,112},{20,12},{24,120},{28,20},{32... | collective-permute-start | bytes 393224 | tf_op jit(solution)/shard_map/ppermute | solution.py:334
  21.5 5.9 %collective-permute-start.4 = (f32[64,128]{1,0:T(8,128)S(1)}, f32[64,128]{1,0:T(8,128)S(1)}, u32[]{:S(2)}, u32[]{:S(2)}) collective-permute-start(f32[64,128]{1,0:T(8,128)S(1)} %get-tuple-element.16), channel_id=1, source_target_pairs={{0,8},{4,36},{8,16},{12,44},{16,24},{20,52},{24,0},{28,60},{32,40}... | collective-permute-start | bytes 98312 | tf_op jit(solution)/shard_map/ppermute | solution.py:340
  23.2 5.4 %collective-permute-start.6 = (f32[64,128]{1,0:T(8,128)S(1)}, f32[64,128]{1,0:T(8,128)S(1)}, u32[]{:S(2)}, u32[]{:S(2)}) collective-permute-start(f32[64,128]{1,0:T(8,128)S(1)} %get-tuple-element.17), channel_id=1, source_target_pairs={{0,16},{4,68},{8,24},{12,76},{16,0},{20,84},{24,8},{28,92},{32,48}... | collective-permute-start | bytes 98312 | tf_op jit(solution)/shard_map/ppermute | solution.py:340
  26.1 3.9 %collective-permute-start.5 = (f32[64,128]{1,0:T(8,128)S(1)}, f32[64,128]{1,0:T(8,128)S(1)}, u32[]{:S(2)}, u32[]{:S(2)}) collective-permute-start(f32[64,128]{1,0:T(8,128)S(1)} %get-tuple-element.18), channel_id=1, source_target_pairs={{0,24},{4,100},{8,0},{12,108},{16,8},{20,116},{24,16},{28,124},{32... | collective-permute-start | bytes 98312 | tf_op jit(solution)/shard_map/ppermute | solution.py:340

commit v6 on v5

--- a/solution.py
+++ b/solution.py
@@ -13,7 +13,7 @@
 INNER = 16
 DEPTH = 256
 CAPACITY = 128
-STEP = 32
+STEP = 64
 AHEAD = 3
 BLOCKS = 32
 
@@ -104,9 +104,11 @@
 def turn_rows(first, blocks, rows, weight, out_ref):
     width = out_ref.shape[1]
 
-    @pl.loop(0, blocks // 4)
+    size = max(n for n in (4, 6, 8) if blocks % n == 0)
+
+    @pl.loop(0, blocks // size)
     def _(group):
-        for b in [4 * group + n for n in range(4)]:
+        for b in [size * group + n for n in range(size)]:
             turned = rows[pl.ds(b * CAPACITY, CAPACITY), :].T
             even = weight[pl.ds(first + b, 1), :]
             odd = weight[pl.ds(BLOCKS + first + b, 1), :]
@@ -168,6 +170,8 @@
             at = slice(j * width + c, j * width + c + 16)
             parts[at, half * LANES:(half + 1) * LANES] = high
             parts[at, DEPTH + half * LANES:DEPTH + (half + 1) * LANES] = low
+        if isinstance(g, int) and g == 0:
+            return
         had[pl.ds(DEPTH + (g >> 8) * 16, 16), :LANES] = low
         x_buf[CHUNKS + (g >> 8), :16, :LANES] = low.astype(jnp.float32)
 

time: 30.8 us -> 30.6 us (level)
  transfers between devices with their start and end apart: 7 -> 7, of which waited for: 4 -> 4; matrix products, arithmetic and copies ran while one was open for 0% -> 0% of each run, Pallas kernels for 12% -> 11%
where the time goes in v6:
time: 30.6 us; the launch traced here: 30.5 us
  Pallas kernels  13.1 us (43%)
  starting transfers between devices  11.7 us (38%)
  waiting for transfers between devices  4.86 us (16%)
  other arithmetic  0.71 us (2%)
    pallas_call x1, Pallas kernels, transform(): pl.pallas_call(transform_kernel, out_shape=(jax.ShapeDtypeStruct((BLOCKS...  9.59 us
    ppermute x3, starting transfers between devices, shards(): lax.ppermute(own[step], 'row', shift(step, False))  5.9 us
    ppermute x3, starting transfers between devices, shards(): lax.ppermute(far[step * 4 - 4:step * 4], 'row', shift(step, True))  5.76 us
    pallas_call x2, Pallas kernels, take(): pl.pallas_call(functools.partial(take_kernel, first), out_shape=jax.Shape...  3.47 us
    ppermute x3, waiting for transfers between devices, shards(): lax.ppermute(own[step], 'row', shift(step, False))  2.56 us
    ppermute x3, waiting for transfers between devices, shards(): lax.ppermute(far[step * 4 - 4:step * 4], 'row', shift(step, True))  2.29 us
    add x1, other arithmetic, shards(): out = out + part  0.62 us
  transfers between devices with their start and end apart: 7, of which 4 were waited for; matrix products, arithmetic and copies ran while one was open for 0% of the time, Pallas kernels for 11%

profile of v6, /device:TPU:0, one launch (start us, length us, event | category | flops | bytes accessed | tf_op | source)
XLA Modules:
  0.0 30.5 jit_solution(16341385104492645316)
XLA Ops:
  0.0 9.6 %shard_map.46 = (f32[16,64,128]{2,1,0:T(8,128)S(1)}, f32[16384,128]{1,0:T(8,128)S(1)}, s32[64,128]{1,0:T(8,128)S(1)}, f32[64,128]{1,0:T(8,128)S(1)}) custom-call(f32[64,32768]{1,0:T(8,128)} %x_ref.1, s32[256,128]{1,0:T(8,128)} %bitcast.17, s32[16,128]{1,0:T(8,128)} %bitcast.18, s32[16,128]{1,0:T(8,128)} %bitcast.19), custom_call_target="tpu_custom_call" | custom-call | tf_op jit(solution)/shard_map/pallas_call | solution.py:256
  9.6 0.1 collective-permute-start
  9.7 2.2 %shard_map.48 = f32[12,64,128]{2,1,0:T(8,128)S(1)} custom-call(f32[16384,128]{1,0:T(8,128)S(1)} %get-tuple-element.9.table, s32[64,128]{1,0:T(8,128)S(1)} %get-tuple-element.10.listed_ref, f32[64,128]{1,0:T(8,128)S(1)} %get-tuple-element.11.weight), custom_call_target="tpu_custom_call" | custom-call | bytes 3145728 | tf_op jit(solution)/shard_map/pallas_call | solution.py:289
  11.9 0.0 collective-permute-done
  12.0 1.6 %collective-permute-start.1 = (f32[4,64,128]{2,1,0:T(8,128)S(1)}, f32[4,64,128]{2,1,0:T(8,128)S(1)}, u32[]{:S(2)}, u32[]{:S(2)}) collective-permute-start(f32[4,64,128]{2,1,0:T(8,128)S(1)} %get-tuple-element.13), channel_id=1, source_target_pairs={{0,32},{4,12},{8,40},{12,20},{16,48},{20,28},{24,56},{28,4},{32,64... | collective-permute-start | bytes 393224 | tf_op jit(solution)/shard_map/ppermute | solution.py:338
  13.6 2.7 %collective-permute-start.3 = (f32[4,64,128]{2,1,0:T(8,128)S(1)}, f32[4,64,128]{2,1,0:T(8,128)S(1)}, u32[]{:S(2)}, u32[]{:S(2)}) collective-permute-start(f32[4,64,128]{2,1,0:T(8,128)S(1)} %get-tuple-element.14), channel_id=1, source_target_pairs={{0,64},{4,20},{8,72},{12,28},{16,80},{20,4},{24,88},{28,12},{32,96... | collective-permute-start | bytes 393224 | tf_op jit(solution)/shard_map/ppermute | solution.py:338
  16.4 1.4 %collective-permute-start.2 = (f32[4,64,128]{2,1,0:T(8,128)S(1)}, f32[4,64,128]{2,1,0:T(8,128)S(1)}, u32[]{:S(2)}, u32[]{:S(2)}) collective-permute-start(f32[4,64,128]{2,1,0:T(8,128)S(1)} %get-tuple-element.15), channel_id=1, source_target_pairs={{0,96},{4,28},{8,104},{12,4},{16,112},{20,12},{24,120},{28,20},{32... | collective-permute-start | bytes 393224 | tf_op jit(solution)/shard_map/ppermute | solution.py:338
  17.8 1.3 %shard_map.47 = f32[4,64,128]{2,1,0:T(8,128)S(1)} custom-call(f32[16384,128]{1,0:T(8,128)S(1)} %get-tuple-element.9.table, s32[64,128]{1,0:T(8,128)S(1)} %get-tuple-element.10.listed_ref, f32[64,128]{1,0:T(8,128)S(1)} %get-tuple-element.11.weight), custom_call_target="tpu_custom_call" | custom-call | bytes 1048576 | tf_op jit(solution)/shard_map/pallas_call | solution.py:289
  19.0 0.0 collective-permute-done.1
  19.1 1.7 %collective-permute-done.3 = f32[4,64,128]{2,1,0:T(8,128)S(1)} collective-permute-done((f32[4,64,128]{2,1,0:T(8,128)S(1)}, f32[4,64,128]{2,1,0:T(8,128)S(1)}, u32[]{:S(2)}, u32[]{:S(2)}) %collective-permute-start.3) | collective-permute-done | bytes 131104 | tf_op jit(solution)/shard_map/ppermute | solution.py:338
  20.7 0.6 %collective-permute-done.2 = f32[4,64,128]{2,1,0:T(8,128)S(1)} collective-permute-done((f32[4,64,128]{2,1,0:T(8,128)S(1)}, f32[4,64,128]{2,1,0:T(8,128)S(1)}, u32[]{:S(2)}, u32[]{:S(2)}) %collective-permute-start.2) | collective-permute-done | bytes 131104 | tf_op jit(solution)/shard_map/ppermute | solution.py:338
  21.4 1.6 %collective-permute-start.4 = (f32[64,128]{1,0:T(8,128)S(1)}, f32[64,128]{1,0:T(8,128)S(1)}, u32[]{:S(2)}, u32[]{:S(2)}) collective-permute-start(f32[64,128]{1,0:T(8,128)S(1)} %get-tuple-element.16), channel_id=1, source_target_pairs={{0,8},{4,36},{8,16},{12,44},{16,24},{20,52},{24,0},{28,60},{32,40}... | collective-permute-start | bytes 98312 | tf_op jit(solution)/shard_map/ppermute | solution.py:344
  23.0 2.9 %collective-permute-start.6 = (f32[64,128]{1,0:T(8,128)S(1)}, f32[64,128]{1,0:T(8,128)S(1)}, u32[]{:S(2)}, u32[]{:S(2)}) collective-permute-start(f32[64,128]{1,0:T(8,128)S(1)} %get-tuple-element.17), channel_id=1, source_target_pairs={{0,16},{4,68},{8,24},{12,76},{16,0},{20,84},{24,8},{28,92},{32,48}... | collective-permute-start | bytes 98312 | tf_op jit(solution)/shard_map/ppermute | solution.py:344
  25.9 1.3 %collective-permute-start.5 = (f32[64,128]{1,0:T(8,128)S(1)}, f32[64,128]{1,0:T(8,128)S(1)}, u32[]{:S(2)}, u32[]{:S(2)}) collective-permute-start(f32[64,128]{1,0:T(8,128)S(1)} %get-tuple-element.18), channel_id=1, source_target_pairs={{0,24},{4,100},{8,0},{12,108},{16,8},{20,116},{24,16},{28,124},{32... | collective-permute-start | bytes 98312 | tf_op jit(solution)/shard_map/ppermute | solution.py:344
  27.3 0.0 collective-permute-done.4
  27.3 1.2 %collective-permute-done.6 = f32[64,128]{1,0:T(8,128)S(1)} collective-permute-done((f32[64,128]{1,0:T(8,128)S(1)}, f32[64,128]{1,0:T(8,128)S(1)}, u32[]{:S(2)}, u32[]{:S(2)}) %collective-permute-start.6) | collective-permute-done | bytes 32800 | tf_op jit(solution)/shard_map/ppermute | solution.py:344
  28.5 1.4 %collective-permute-done.5 = f32[64,128]{1,0:T(8,128)S(1)} collective-permute-done((f32[64,128]{1,0:T(8,128)S(1)}, f32[64,128]{1,0:T(8,128)S(1)}, u32[]{:S(2)}, u32[]{:S(2)}) %collective-permute-start.5) | collective-permute-done | bytes 32800 | tf_op jit(solution)/shard_map/ppermute | solution.py:344
  29.9 0.6 %fusion.5 = f32[64,128]{1,0:T(8,128)} fusion(f32[64,128]{1,0:T(8,128)S(1)} %collective-permute-done.6, f32[64,128]{1,0:T(8,128)S(1)} %collective-permute-done.5, f32[64,128]{1,0:T(8,128)S(1)} %collective-permute-done.4, f32[4,64,128]{2,1,0:T(8,128)S(1)} %fusion.2), kind=kLoop, calls=%fused_computation.11 | loop fusion | flops 24576 | bytes 163840 | tf_op jit(solution)/shard_map/add | solution.py:347
  (4 shorter events, 0.1 us)
Async XLA Ops:
  9.6 2.3 %collective-permute-start = (f32[16,64,128]{2,1,0:T(8,128)S(1)}, f32[16,64,128]{2,1,0:T(8,128)S(1)}, u32[]{:S(2)}, u32[]{:S(2)}) collective-permute-start(f32[16,64,128]{2,1,0:T(8,128)S(1)} %get-tuple-element.12), channel_id=1, source_target_pairs={{0,4},{4,0},{8,12},{12,8},{16,20},{20,16},{24,28},{28,24},{32,36},... | collective-permute-start | bytes 1572872 | tf_op jit(solution)/shard_map/ppermute | solution.py:335
  12.0 7.0 %collective-permute-start.1 = (f32[4,64,128]{2,1,0:T(8,128)S(1)}, f32[4,64,128]{2,1,0:T(8,128)S(1)}, u32[]{:S(2)}, u32[]{:S(2)}) collective-permute-start(f32[4,64,128]{2,1,0:T(8,128)S(1)} %get-tuple-element.13), channel_id=1, source_target_pairs={{0,32},{4,12},{8,40},{12,20},{16,48},{20,28},{24,56},{28,4},{32,64... | collective-permute-start | bytes 393224 | tf_op jit(solution)/shard_map/ppermute | solution.py:338
  13.6 7.1 %collective-permute-start.3 = (f32[4,64,128]{2,1,0:T(8,128)S(1)}, f32[4,64,128]{2,1,0:T(8,128)S(1)}, u32[]{:S(2)}, u32[]{:S(2)}) collective-permute-start(f32[4,64,128]{2,1,0:T(8,128)S(1)} %get-tuple-element.14), channel_id=1, source_target_pairs={{0,64},{4,20},{8,72},{12,28},{16,80},{20,4},{24,88},{28,12},{32,96... | collective-permute-start | bytes 393224 | tf_op jit(solution)/shard_map/ppermute | solution.py:338
  16.4 5.0 %collective-permute-start.2 = (f32[4,64,128]{2,1,0:T(8,128)S(1)}, f32[4,64,128]{2,1,0:T(8,128)S(1)}, u32[]{:S(2)}, u32[]{:S(2)}) collective-permute-start(f32[4,64,128]{2,1,0:T(8,128)S(1)} %get-tuple-element.15), channel_id=1, source_target_pairs={{0,96},{4,28},{8,104},{12,4},{16,112},{20,12},{24,120},{28,20},{32... | collective-permute-start | bytes 393224 | tf_op jit(solution)/shard_map/ppermute | solution.py:338
  21.4 5.9 %collective-permute-start.4 = (f32[64,128]{1,0:T(8,128)S(1)}, f32[64,128]{1,0:T(8,128)S(1)}, u32[]{:S(2)}, u32[]{:S(2)}) collective-permute-start(f32[64,128]{1,0:T(8,128)S(1)} %get-tuple-element.16), channel_id=1, source_target_pairs={{0,8},{4,36},{8,16},{12,44},{16,24},{20,52},{24,0},{28,60},{32,40}... | collective-permute-start | bytes 98312 | tf_op jit(solution)/shard_map/ppermute | solution.py:344
  23.0 5.4 %collective-permute-start.6 = (f32[64,128]{1,0:T(8,128)S(1)}, f32[64,128]{1,0:T(8,128)S(1)}, u32[]{:S(2)}, u32[]{:S(2)}) collective-permute-start(f32[64,128]{1,0:T(8,128)S(1)} %get-tuple-element.17), channel_id=1, source_target_pairs={{0,16},{4,68},{8,24},{12,76},{16,0},{20,84},{24,8},{28,92},{32,48}... | collective-permute-start | bytes 98312 | tf_op jit(solution)/shard_map/ppermute | solution.py:344
  25.9 3.9 %collective-permute-start.5 = (f32[64,128]{1,0:T(8,128)S(1)}, f32[64,128]{1,0:T(8,128)S(1)}, u32[]{:S(2)}, u32[]{:S(2)}) collective-permute-start(f32[64,128]{1,0:T(8,128)S(1)} %get-tuple-element.18), channel_id=1, source_target_pairs={{0,24},{4,100},{8,0},{12,108},{16,8},{20,116},{24,16},{28,124},{32... | collective-permute-start | bytes 98312 | tf_op jit(solution)/shard_map/ppermute | solution.py:344

commit v7 on v6

--- a/solution.py
+++ b/solution.py
@@ -219,7 +219,7 @@
     stretch = table.shape[0] // 16
     step = 16
 
-    @pl.loop(0, stretch // step, unroll=2)
+    @pl.loop(0, stretch // step, unroll=4)
     def _(at):
         values = [table[pl.ds(g * stretch + at * step, step), :] for g in range(16)]
         for g, value in enumerate(butterflies(values)):

time: 30.6 us -> 30.4 us (level)
  no operation moved by 1% of the time
where the time goes in v7:
time: 30.4 us; the launch traced here: 30.3 us
  Pallas kernels  12.8 us (42%)
  starting transfers between devices  11.8 us (39%)
  waiting for transfers between devices  4.81 us (16%)
  other arithmetic  0.71 us (2%)
    pallas_call x1, Pallas kernels, transform(): pl.pallas_call(transform_kernel, out_shape=(jax.ShapeDtypeStruct((BLOCKS...  9.36 us
    ppermute x3, starting transfers between devices, shards(): lax.ppermute(own[step], 'row', shift(step, False))  5.9 us
    ppermute x3, starting transfers between devices, shards(): lax.ppermute(far[step * 4 - 4:step * 4], 'row', shift(step, True))  5.81 us
    pallas_call x2, Pallas kernels, take(): pl.pallas_call(functools.partial(take_kernel, first), out_shape=jax.Shape...  3.47 us
    ppermute x3, waiting for transfers between devices, shards(): lax.ppermute(own[step], 'row', shift(step, False))  2.56 us
    ppermute x3, waiting for transfers between devices, shards(): lax.ppermute(far[step * 4 - 4:step * 4], 'row', shift(step, True))  2.24 us
    add x1, other arithmetic, shards(): out = out + part  0.62 us
  transfers between devices with their start and end apart: 7, of which 4 were waited for; matrix products, arithmetic and copies ran while one was open for 0% of the time, Pallas kernels for 11%

profile of v7, /device:TPU:0, one launch (start us, length us, event | category | flops | bytes accessed | tf_op | source)
XLA Modules:
  0.0 30.3 jit_solution(6948241053651794303)
XLA Ops:
  0.0 9.4 %shard_map.46 = (f32[16,64,128]{2,1,0:T(8,128)S(1)}, f32[16384,128]{1,0:T(8,128)S(1)}, s32[64,128]{1,0:T(8,128)S(1)}, f32[64,128]{1,0:T(8,128)S(1)}) custom-call(f32[64,32768]{1,0:T(8,128)} %x_ref.1, s32[256,128]{1,0:T(8,128)} %bitcast.17, s32[16,128]{1,0:T(8,128)} %bitcast.18, s32[16,128]{1,0:T(8,128)} %bitcast.19), custom_call_target="tpu_custom_call" | custom-call | tf_op jit(solution)/shard_map/pallas_call | solution.py:256
  9.4 0.1 collective-permute-start
  9.5 2.2 %shard_map.48 = f32[12,64,128]{2,1,0:T(8,128)S(1)} custom-call(f32[16384,128]{1,0:T(8,128)S(1)} %get-tuple-element.9.table, s32[64,128]{1,0:T(8,128)S(1)} %get-tuple-element.10.listed_ref, f32[64,128]{1,0:T(8,128)S(1)} %get-tuple-element.11.weight), custom_call_target="tpu_custom_call" | custom-call | bytes 3145728 | tf_op jit(solution)/shard_map/pallas_call | solution.py:289
  11.7 0.0 collective-permute-done
  11.8 1.4 %collective-permute-start.1 = (f32[4,64,128]{2,1,0:T(8,128)S(1)}, f32[4,64,128]{2,1,0:T(8,128)S(1)}, u32[]{:S(2)}, u32[]{:S(2)}) collective-permute-start(f32[4,64,128]{2,1,0:T(8,128)S(1)} %get-tuple-element.13), channel_id=1, source_target_pairs={{0,32},{4,12},{8,40},{12,20},{16,48},{20,28},{24,56},{28,4},{32,64... | collective-permute-start | bytes 393224 | tf_op jit(solution)/shard_map/ppermute | solution.py:338
  13.3 2.9 %collective-permute-start.3 = (f32[4,64,128]{2,1,0:T(8,128)S(1)}, f32[4,64,128]{2,1,0:T(8,128)S(1)}, u32[]{:S(2)}, u32[]{:S(2)}) collective-permute-start(f32[4,64,128]{2,1,0:T(8,128)S(1)} %get-tuple-element.14), channel_id=1, source_target_pairs={{0,64},{4,20},{8,72},{12,28},{16,80},{20,4},{24,88},{28,12},{32,96... | collective-permute-start | bytes 393224 | tf_op jit(solution)/shard_map/ppermute | solution.py:338
  16.1 1.5 %collective-permute-start.2 = (f32[4,64,128]{2,1,0:T(8,128)S(1)}, f32[4,64,128]{2,1,0:T(8,128)S(1)}, u32[]{:S(2)}, u32[]{:S(2)}) collective-permute-start(f32[4,64,128]{2,1,0:T(8,128)S(1)} %get-tuple-element.15), channel_id=1, source_target_pairs={{0,96},{4,28},{8,104},{12,4},{16,112},{20,12},{24,120},{28,20},{32... | collective-permute-start | bytes 393224 | tf_op jit(solution)/shard_map/ppermute | solution.py:338
  17.6 1.2 %shard_map.47 = f32[4,64,128]{2,1,0:T(8,128)S(1)} custom-call(f32[16384,128]{1,0:T(8,128)S(1)} %get-tuple-element.9.table, s32[64,128]{1,0:T(8,128)S(1)} %get-tuple-element.10.listed_ref, f32[64,128]{1,0:T(8,128)S(1)} %get-tuple-element.11.weight), custom_call_target="tpu_custom_call" | custom-call | bytes 1048576 | tf_op jit(solution)/shard_map/pallas_call | solution.py:289
  18.9 0.0 collective-permute-done.1
  18.9 1.6 %collective-permute-done.3 = f32[4,64,128]{2,1,0:T(8,128)S(1)} collective-permute-done((f32[4,64,128]{2,1,0:T(8,128)S(1)}, f32[4,64,128]{2,1,0:T(8,128)S(1)}, u32[]{:S(2)}, u32[]{:S(2)}) %collective-permute-start.3) | collective-permute-done | bytes 131104 | tf_op jit(solution)/shard_map/ppermute | solution.py:338
  20.5 0.6 %collective-permute-done.2 = f32[4,64,128]{2,1,0:T(8,128)S(1)} collective-permute-done((f32[4,64,128]{2,1,0:T(8,128)S(1)}, f32[4,64,128]{2,1,0:T(8,128)S(1)}, u32[]{:S(2)}, u32[]{:S(2)}) %collective-permute-start.2) | collective-permute-done | bytes 131104 | tf_op jit(solution)/shard_map/ppermute | solution.py:338
  21.2 1.6 %collective-permute-start.4 = (f32[64,128]{1,0:T(8,128)S(1)}, f32[64,128]{1,0:T(8,128)S(1)}, u32[]{:S(2)}, u32[]{:S(2)}) collective-permute-start(f32[64,128]{1,0:T(8,128)S(1)} %get-tuple-element.16), channel_id=1, source_target_pairs={{0,8},{4,36},{8,16},{12,44},{16,24},{20,52},{24,0},{28,60},{32,40}... | collective-permute-start | bytes 98312 | tf_op jit(solution)/shard_map/ppermute | solution.py:344
  22.8 2.9 %collective-permute-start.6 = (f32[64,128]{1,0:T(8,128)S(1)}, f32[64,128]{1,0:T(8,128)S(1)}, u32[]{:S(2)}, u32[]{:S(2)}) collective-permute-start(f32[64,128]{1,0:T(8,128)S(1)} %get-tuple-element.17), channel_id=1, source_target_pairs={{0,16},{4,68},{8,24},{12,76},{16,0},{20,84},{24,8},{28,92},{32,48}... | collective-permute-start | bytes 98312 | tf_op jit(solution)/shard_map/ppermute | solution.py:344
  25.7 1.3 %collective-permute-start.5 = (f32[64,128]{1,0:T(8,128)S(1)}, f32[64,128]{1,0:T(8,128)S(1)}, u32[]{:S(2)}, u32[]{:S(2)}) collective-permute-start(f32[64,128]{1,0:T(8,128)S(1)} %get-tuple-element.18), channel_id=1, source_target_pairs={{0,24},{4,100},{8,0},{12,108},{16,8},{20,116},{24,16},{28,124},{32... | collective-permute-start | bytes 98312 | tf_op jit(solution)/shard_map/ppermute | solution.py:344
  27.1 0.0 collective-permute-done.4
  27.1 1.2 %collective-permute-done.6 = f32[64,128]{1,0:T(8,128)S(1)} collective-permute-done((f32[64,128]{1,0:T(8,128)S(1)}, f32[64,128]{1,0:T(8,128)S(1)}, u32[]{:S(2)}, u32[]{:S(2)}) %collective-permute-start.6) | collective-permute-done | bytes 32800 | tf_op jit(solution)/shard_map/ppermute | solution.py:344
  28.2 1.4 %collective-permute-done.5 = f32[64,128]{1,0:T(8,128)S(1)} collective-permute-done((f32[64,128]{1,0:T(8,128)S(1)}, f32[64,128]{1,0:T(8,128)S(1)}, u32[]{:S(2)}, u32[]{:S(2)}) %collective-permute-start.5) | collective-permute-done | bytes 32800 | tf_op jit(solution)/shard_map/ppermute | solution.py:344
  29.6 0.6 %fusion.5 = f32[64,128]{1,0:T(8,128)} fusion(f32[64,128]{1,0:T(8,128)S(1)} %collective-permute-done.6, f32[64,128]{1,0:T(8,128)S(1)} %collective-permute-done.5, f32[64,128]{1,0:T(8,128)S(1)} %collective-permute-done.4, f32[4,64,128]{2,1,0:T(8,128)S(1)} %fusion.2), kind=kLoop, calls=%fused_computation.11 | loop fusion | flops 24576 | bytes 163840 | tf_op jit(solution)/shard_map/add | solution.py:347
  (4 shorter events, 0.1 us)
Async XLA Ops:
  9.4 2.4 %collective-permute-start = (f32[16,64,128]{2,1,0:T(8,128)S(1)}, f32[16,64,128]{2,1,0:T(8,128)S(1)}, u32[]{:S(2)}, u32[]{:S(2)}) collective-permute-start(f32[16,64,128]{2,1,0:T(8,128)S(1)} %get-tuple-element.12), channel_id=1, source_target_pairs={{0,4},{4,0},{8,12},{12,8},{16,20},{20,16},{24,28},{28,24},{32,36},... | collective-permute-start | bytes 1572872 | tf_op jit(solution)/shard_map/ppermute | solution.py:335
  11.8 7.0 %collective-permute-start.1 = (f32[4,64,128]{2,1,0:T(8,128)S(1)}, f32[4,64,128]{2,1,0:T(8,128)S(1)}, u32[]{:S(2)}, u32[]{:S(2)}) collective-permute-start(f32[4,64,128]{2,1,0:T(8,128)S(1)} %get-tuple-element.13), channel_id=1, source_target_pairs={{0,32},{4,12},{8,40},{12,20},{16,48},{20,28},{24,56},{28,4},{32,64... | collective-permute-start | bytes 393224 | tf_op jit(solution)/shard_map/ppermute | solution.py:338
  13.3 7.2 %collective-permute-start.3 = (f32[4,64,128]{2,1,0:T(8,128)S(1)}, f32[4,64,128]{2,1,0:T(8,128)S(1)}, u32[]{:S(2)}, u32[]{:S(2)}) collective-permute-start(f32[4,64,128]{2,1,0:T(8,128)S(1)} %get-tuple-element.14), channel_id=1, source_target_pairs={{0,64},{4,20},{8,72},{12,28},{16,80},{20,4},{24,88},{28,12},{32,96... | collective-permute-start | bytes 393224 | tf_op jit(solution)/shard_map/ppermute | solution.py:338
  16.1 5.0 %collective-permute-start.2 = (f32[4,64,128]{2,1,0:T(8,128)S(1)}, f32[4,64,128]{2,1,0:T(8,128)S(1)}, u32[]{:S(2)}, u32[]{:S(2)}) collective-permute-start(f32[4,64,128]{2,1,0:T(8,128)S(1)} %get-tuple-element.15), channel_id=1, source_target_pairs={{0,96},{4,28},{8,104},{12,4},{16,112},{20,12},{24,120},{28,20},{32... | collective-permute-start | bytes 393224 | tf_op jit(solution)/shard_map/ppermute | solution.py:338
  21.2 5.9 %collective-permute-start.4 = (f32[64,128]{1,0:T(8,128)S(1)}, f32[64,128]{1,0:T(8,128)S(1)}, u32[]{:S(2)}, u32[]{:S(2)}) collective-permute-start(f32[64,128]{1,0:T(8,128)S(1)} %get-tuple-element.16), channel_id=1, source_target_pairs={{0,8},{4,36},{8,16},{12,44},{16,24},{20,52},{24,0},{28,60},{32,40}... | collective-permute-start | bytes 98312 | tf_op jit(solution)/shard_map/ppermute | solution.py:344
  22.8 5.4 %collective-permute-start.6 = (f32[64,128]{1,0:T(8,128)S(1)}, f32[64,128]{1,0:T(8,128)S(1)}, u32[]{:S(2)}, u32[]{:S(2)}) collective-permute-start(f32[64,128]{1,0:T(8,128)S(1)} %get-tuple-element.17), channel_id=1, source_target_pairs={{0,16},{4,68},{8,24},{12,76},{16,0},{20,84},{24,8},{28,92},{32,48}... | collective-permute-start | bytes 98312 | tf_op jit(solution)/shard_map/ppermute | solution.py:344
  25.7 3.9 %collective-permute-start.5 = (f32[64,128]{1,0:T(8,128)S(1)}, f32[64,128]{1,0:T(8,128)S(1)}, u32[]{:S(2)}, u32[]{:S(2)}) collective-permute-start(f32[64,128]{1,0:T(8,128)S(1)} %get-tuple-element.18), channel_id=1, source_target_pairs={{0,24},{4,100},{8,0},{12,108},{16,8},{20,116},{24,16},{28,124},{32... | collective-permute-start | bytes 98312 | tf_op jit(solution)/shard_map/ppermute | solution.py:344
